TPU v7x, 32 devices: a whole 2x2x4 slice. The times are simulated.
32 devices in a mesh: dp: 16 (over z, y, x), own: 2 (over core).
Axes of the slice: x: 2, y: 2, z: 4, core: 2. Of those that a mesh axis runs over, the one named last changes fastest.
Arguments:
- tokens: bfloat16 [16384, 1024], P(('dp', 'own')), may hold values from -6 to 6
- cotangent: bfloat16 [16384, 1024], P(('dp', 'own')), may hold values from -6 to 6
- slot_table: int32 [12], replicated, may hold values from 0 to 11, as said below
- matrix_master: float32 [12, 1024, 1024], P('own')
- matrix_momentum: float32 [12, 1024, 1024], P('own')
- vector_params: float32 [12, 1024], replicated
- vector_first: float32 [12, 1024], replicated
- vector_second: float32 [12, 1024], replicated, as said below
Outputs:
- activations: float32 [16384, 1024], P(('dp', 'own'))
- input_grad: float32 [16384, 1024], P(('dp', 'own'))
- new_master: float32 [12, 1024, 1024], P('own')
- new_momentum: float32 [12, 1024, 1024], P('own')
- new_vector_params: float32 [12, 1024], replicated
- new_vector_first: float32 [12, 1024], replicated
- new_vector_second: float32 [12, 1024], replicated
Inputs may be any that keep to these rules, and one draw needn't show every extreme that they name: Block b (query, key, value, output projection, then the 4 column blocks of the up projection, then the 4 row blocks of the down projection) lives in slot slot_table[b]; the values are distinct and slot 11 is always named. `vector_second`: positive.
All inputs are finite; a program needn't handle non-finite values.
Results may differ from a plain program's by a relative error of at most 0.035.
Values may be sent and summed in bfloat16 or wider, within the bound.
A program may use at most 384 MiB of HBM per device.

v0:
```python
import math

import jax
import jax.numpy as jnp
from jax import lax
from jax.sharding import PartitionSpec as P

HEADS = 16
HEAD = 64
LEN = 512
NEWTON_STEPS = 5
STEP = 10


poly_first = 3.4445
poly_second = -4.775
poly_third = 2.0315
momentum_decay = 0.95
matrix_rate = 1.0
matrix_decay = 0.01
beta_first = 0.9
beta_second = 0.999
vector_rate = 0.2
vector_decay = 0.01
adam_epsilon = 1e-08
norm_epsilon = 1e-05
ortho_epsilon = 1e-07


def layer_norm(values, gain_row, shift_row):
    centred = values - jnp.mean(values, axis=-1, keepdims=True)
    spread = jnp.mean(centred * centred, axis=-1, keepdims=True)
    return centred * lax.rsqrt(spread + norm_epsilon) * gain_row + shift_row


def gelu_exact(values):
    return 0.5 * values * (1.0 + jax.scipy.special.erf(values * (1.0 / math.sqrt(2.0))))


def contract_last(operand_left, operand_right):
    return lax.dot_general(
        operand_left, operand_right, (((1,), (1,)), ((), ())), preferred_element_type=jnp.float32
    )


def contract_first(operand_left, operand_right):
    return lax.dot_general(
        operand_left, operand_right, (((0,), (0,)), ((), ())), preferred_element_type=jnp.float32
    )


def head_scores(queries, key_rows):
    length = queries.shape[0]
    query_heads = queries.reshape(length, HEADS, HEAD)
    key_heads = key_rows.reshape(length, HEADS, HEAD)
    scores = jnp.einsum("qhd,khd->hqk", query_heads, key_heads, preferred_element_type=jnp.float32)
    return (scores * (1.0 / math.sqrt(HEAD)), query_heads, key_heads)


def attend_forward(triple):
    queries, key_rows, values = triple
    length = queries.shape[0]
    scores, query_heads, key_heads = head_scores(queries, key_rows)
    row_peak = jnp.max(scores, axis=-1, keepdims=True)
    exps = jnp.exp(scores - row_peak)
    row_total = jnp.sum(exps, axis=-1, keepdims=True)
    probabilities = (exps / row_total).astype(jnp.bfloat16)
    value_heads = values.reshape(length, HEADS, HEAD)
    mixed = jnp.einsum(
        "hqk,khd->qhd", probabilities, value_heads, preferred_element_type=jnp.float32
    )
    return (mixed.reshape(length, HEADS * HEAD).astype(jnp.bfloat16), row_peak, row_total)


def attend_backward(bundle):
    queries, key_rows, values, grad_mixed, row_peak, row_total = bundle
    length = queries.shape[0]
    scores, query_heads, key_heads = head_scores(queries, key_rows)
    probabilities = jnp.exp(scores - row_peak) / row_total
    value_heads = values.reshape(length, HEADS, HEAD)
    grad_heads = grad_mixed.reshape(length, HEADS, HEAD)
    grad_probs = jnp.einsum(
        "qhd,khd->hqk", grad_heads, value_heads, preferred_element_type=jnp.float32
    )
    row_dot = jnp.sum(grad_probs * probabilities, axis=-1, keepdims=True)
    grad_scores = (probabilities * (grad_probs - row_dot)).astype(jnp.bfloat16)
    scale = 1.0 / math.sqrt(HEAD)
    grad_query = (
        jnp.einsum("hqk,khd->qhd", grad_scores, key_heads, preferred_element_type=jnp.float32)
        * scale
    )
    grad_key = (
        jnp.einsum("hqk,qhd->khd", grad_scores, query_heads, preferred_element_type=jnp.float32)
        * scale
    )
    grad_value = jnp.einsum(
        "hqk,qhd->khd",
        probabilities.astype(jnp.bfloat16),
        grad_heads,
        preferred_element_type=jnp.float32,
    )
    features = HEADS * HEAD
    joined = jnp.concatenate(
        [
            grad_query.reshape(length, features),
            grad_key.reshape(length, features),
            grad_value.reshape(length, features),
        ],
        axis=1,
    )
    return joined.astype(jnp.bfloat16)


def orthogonal(momentum):
    iterate = momentum / (jnp.sqrt(jnp.sum(momentum * momentum)) + ortho_epsilon)
    for sweep in range(NEWTON_STEPS):
        low_iter = iterate.astype(jnp.bfloat16)
        gram = contract_last(low_iter, low_iter)
        gram_low = gram.astype(jnp.bfloat16)
        square = jnp.dot(gram_low, gram_low, preferred_element_type=jnp.float32)
        poly = (poly_second * gram + poly_third * square).astype(jnp.bfloat16)
        iterate = poly_first * iterate + jnp.dot(poly, low_iter, preferred_element_type=jnp.float32)
    return iterate


def empty_result(momentum):
    return jnp.zeros_like(momentum)


def on_device(
    tokens,
    cotangent,
    slot_table,
    matrix_master,
    matrix_momentum,
    vector_params,
    vector_first,
    vector_second,
):
    features = tokens.shape[1]
    hidden_blocks = vector_params.shape[0] - 8
    slots = matrix_master.shape[0]
    owners = lax.axis_size("own")
    slot_count = slots * owners
    gathered = lax.all_gather(matrix_master.astype(jnp.bfloat16), "own", axis=0, tiled=True)
    blocks = jnp.take(gathered, slot_table, axis=0)
    w_qkv = blocks[0:3].transpose(1, 0, 2).reshape(features, 3 * features)
    w_out = blocks[3]
    w_up = (
        blocks[4 : 4 + hidden_blocks].transpose(1, 0, 2).reshape(features, hidden_blocks * features)
    )
    w_down = blocks[4 + hidden_blocks :].reshape(hidden_blocks * features, features)
    bias_qkv = jnp.concatenate(
        [vector_params[0], jnp.zeros((features,), jnp.float32), vector_params[1]]
    )
    bias_up = vector_params[8:].reshape(hidden_blocks * features)
    qkv = (jnp.dot(tokens, w_qkv, preferred_element_type=jnp.float32) + bias_qkv).astype(
        jnp.bfloat16
    )
    sequences = tokens.shape[0] // LEN
    split_qkv = qkv.reshape(sequences, LEN, 3, features)
    triples = (split_qkv[:, :, 0], split_qkv[:, :, 1], split_qkv[:, :, 2])
    mixed_rows, row_peak, row_total = lax.map(attend_forward, triples)
    mixed_rows = mixed_rows.reshape(sequences * LEN, features)
    attn_out = jnp.dot(mixed_rows, w_out, preferred_element_type=jnp.float32) + vector_params[2]
    normed, norm_one_back = jax.vjp(
        layer_norm, tokens.astype(jnp.float32) + attn_out, vector_params[4], vector_params[5]
    )
    normed_low = normed.astype(jnp.bfloat16)
    pre_hidden = jnp.dot(normed_low, w_up, preferred_element_type=jnp.float32) + bias_up
    activity_full, gelu_back = jax.vjp(gelu_exact, pre_hidden)
    activity = activity_full.astype(jnp.bfloat16)
    branch = jnp.dot(activity, w_down, preferred_element_type=jnp.float32) + vector_params[3]
    output, norm_two_back = jax.vjp(layer_norm, normed + branch, vector_params[6], vector_params[7])
    d_resid_two, d_gain_two, d_shift_two = norm_two_back(cotangent.astype(jnp.float32))
    d_branch = d_resid_two.astype(jnp.bfloat16)
    d_activity = contract_last(d_branch, w_down)
    (d_pre,) = gelu_back(d_activity)
    d_hidden = d_pre.astype(jnp.bfloat16)
    d_normed = d_resid_two + contract_last(d_hidden, w_up)
    d_resid_one, d_gain_one, d_shift_one = norm_one_back(d_normed)
    d_attn = d_resid_one.astype(jnp.bfloat16)
    d_mixed = contract_last(d_attn, w_out).astype(jnp.bfloat16)
    bundle = (
        triples[0],
        triples[1],
        triples[2],
        d_mixed.reshape(sequences, LEN, features),
        row_peak,
        row_total,
    )
    d_qkv = lax.map(attend_backward, bundle).reshape(sequences * LEN, 3 * features)
    input_grad = d_resid_one + contract_last(d_qkv, w_qkv)
    column_sums = jnp.sum(d_qkv, axis=0, dtype=jnp.float32)
    vector_local = jnp.concatenate(
        [
            jnp.stack(
                [
                    column_sums[:features],
                    column_sums[2 * features :],
                    jnp.sum(d_attn, axis=0, dtype=jnp.float32),
                    jnp.sum(d_branch, axis=0, dtype=jnp.float32),
                    d_gain_one,
                    d_shift_one,
                    d_gain_two,
                    d_shift_two,
                ]
            ),
            jnp.sum(d_hidden, axis=0, dtype=jnp.float32).reshape(hidden_blocks, features),
        ],
        axis=0,
    )
    vector_grad = lax.psum(vector_local, ("dp", "own"))
    grad_qkv = contract_first(tokens, d_qkv)
    grad_out = contract_first(mixed_rows, d_attn)
    grad_up = contract_first(normed_low, d_hidden)
    grad_down = contract_first(activity, d_branch)
    grad_blocks = jnp.concatenate(
        [
            grad_qkv.reshape(features, 3, features).transpose(1, 0, 2),
            grad_out[None],
            grad_up.reshape(features, hidden_blocks, features).transpose(1, 0, 2),
            grad_down.reshape(hidden_blocks, features, features),
        ],
        axis=0,
    )
    match = slot_table[None, :] == jnp.arange(slot_count, dtype=jnp.int32)[:, None]
    slot_used = jnp.any(match, axis=1)
    block_index = jnp.sum(
        jnp.where(match, jnp.arange(slot_table.shape[0], dtype=jnp.int32)[None, :], 0), axis=1
    )
    slot_grad = jnp.where(slot_used[:, None, None], jnp.take(grad_blocks, block_index, axis=0), 0.0)
    data_count = lax.axis_size("dp")
    piece_rows = features // data_count
    arranged = slot_grad.reshape(owners, slots, data_count, piece_rows, features).transpose(
        2, 0, 1, 3, 4
    )
    arranged = arranged.reshape(data_count * owners, slots, piece_rows, features)
    share = lax.psum_scatter(arranged, ("dp", "own"), scatter_dimension=0, tiled=True)
    gathered_rows = lax.all_gather(share.astype(jnp.bfloat16), "dp", axis=0, tiled=True).astype(
        share.dtype
    )
    summed = gathered_rows.transpose(1, 0, 2, 3).reshape(slots, features, features)
    new_momentum = momentum_decay * matrix_momentum + summed
    used_here = lax.dynamic_slice_in_dim(slot_used, lax.axis_index("own") * slots, slots)
    ortho = jnp.stack(
        [
            lax.cond(used_here[slot_place], orthogonal, empty_result, new_momentum[slot_place])
            for slot_place in range(slots)
        ]
    )
    new_master = matrix_master - matrix_rate * (ortho + matrix_decay * matrix_master)
    new_first = beta_first * vector_first + (1.0 - beta_first) * vector_grad
    new_second = beta_second * vector_second + (1.0 - beta_second) * vector_grad * vector_grad
    first_hat = new_first / (1.0 - beta_first**STEP)
    second_hat = new_second / (1.0 - beta_second**STEP)
    new_params = vector_params - vector_rate * (
        first_hat / (jnp.sqrt(second_hat) + adam_epsilon) + vector_decay * vector_params
    )
    return (output, input_grad, new_master, new_momentum, new_params, new_first, new_second)


def solution(mesh):
    in_specs = (
        P(("dp", "own"), None),
        P(("dp", "own"), None),
        P(),
        P("own", None, None),
        P("own", None, None),
        P(),
        P(),
        P(),
    )
    out_specs = (
        P(("dp", "own"), None),
        P(("dp", "own"), None),
        P("own", None, None),
        P("own", None, None),
        P(),
        P(),
        P(),
    )
    return jax.shard_map(
        on_device, mesh=mesh, in_specs=in_specs, out_specs=out_specs, check_vma=False
    )
```

profile of v0, /device:TPU:0, one launch (start us, length us, event | category | flops | bytes accessed | tf_op | source)
XLA Modules:
  0.0 1890.2 jit_solution(3784336735822784514)
XLA Ops:
  24.5 39.2 %all-gather.3.cloned.1.call-done = bf16[12,1024,1024]{2,1,0:T(8,128)(2,1)} async-done(((bf16[6,1024,1024]{2,1,0:T(8,128)(2,1)}), bf16[12,1024,1024]{2,1,0:T(8,128)(2,1)}) %all-gather.3.cloned.1.call-update) | async-done | bytes 25165840 | tf_op jit(solution)/shard_map/all_gather | solution.py:145
  63.7 17.5 fusion.317
  102.3 23.1 %maximum_select_fusion = bf16[12,1024,1024]{2,1,0:T(8,128)(2,1)} fusion(bf16[12,512,1024]{2,1,0:T(8,128)(2,1)} %gather_fusion.1, bf16[12,512,1024]{2,1,0:T(8,128)(2,1)} %gather_fusion, pred[12]{0:T(512)(128)(4,1)S(1)} %compare_and_fusion.1), kind=kLoop, calls=%fused_computation.272 | loop fusion | flops 62914560 | bytes 50331660 | tf_op jit(solution)/shard_map/jit(_take)/select_n | solution.py:146
  330.8 33.2 %pad_maximum_fusion = f32[12,1024,1024]{2,1,0:T(8,128)} fusion(f32[4,1024,1024]{2,1,0:T(8,128)} %bitcast.192, f32[4,1024,1024]{2,1,0:T(8,128)} %bitcast.187, f32[1,1024,1024]{2,1,0:T(8,128)} %convolution_bitcast_fusion, f32[3,1024,1024]{2,1,0:T(8,128)} %bitcast.188), kind=kLoop, calls=%fused_computation.269 | loop fusion | flops 37748736 | bytes 100663296 | tf_op jit(solution)/shard_map/concatenate | solution.py:218
  364.1 33.1 %fusion.315 = (f32[12,512,1024]{2,1,0:T(8,128)}, f32[12,512,1024]{2,1,0:T(8,128)}) fusion(f32[12,1024,1024]{2,1,0:T(8,128)} %pad_maximum_fusion), kind=kLoop, calls=%fused_computation.371 | loop fusion | bytes 100663296 | tf_op jit(solution)/shard_map/jit(_take)/gather | solution.py:232
  397.1 18.8 gather_fusion.2
  415.9 19.2 %gather_fusion.3 = f32[12,512,1024]{2,1,0:T(8,128)} fusion(f32[12,512,1024]{2,1,0:T(8,128)} %get-tuple-element.114, s32[1024]{0:T(1024)} %pad_clamp_fusion), kind=kCustom, calls=%fused_computation.3 | custom fusion | bytes 50331696 | tf_op jit(solution)/shard_map/jit(_take)/gather | solution.py:232
  435.1 33.5 %pad_maximum_fusion.1 = f32[12,1024,1024]{2,1,0:T(8,128)} fusion(f32[12,512,1024]{2,1,0:T(8,128)} %gather_fusion.3, f32[12,512,1024]{2,1,0:T(8,128)} %gather_fusion.2), kind=kLoop, calls=%fused_computation.270 | loop fusion | flops 12582912 | bytes 100663296
  468.6 36.9 %select_bitcast_fusion = f32[16,2,6,64,1024]{4,3,0,2,1:T(8,128)} fusion(f32[2,6,16,64,1024]{4,3,2,1,0:T(8,128)} %bitcast.186, pred[2,6]{1,0:T(4,128)(4,1)S(1)} %copy-done.43, pred[2,6]{1,0:T(4,128)(4,1)S(1)} %copy-done.42), kind=kLoop, calls=%fused_computation.271 | loop fusion | flops 25165824 | bytes 100663320 | tf_op jit(solution)/shard_map/transpose | solution.py:235
  505.5 34.9 %copy.73 = f32[16,2,6,64,1024]{4,3,2,1,0:T(8,128)} copy(f32[16,2,6,64,1024]{4,3,0,2,1:T(8,128)} %select_bitcast_fusion) | data formatting | bytes 100663296 | tf_op jit(solution)/shard_map/transpose | solution.py:235
  540.6 432.7 %reduce-scatter.2.cloned.1.call-done = f32[1,6,64,1024]{3,2,1,0:T(8,128)} async-done(((f32[32,6,64,1024]{3,2,1,0:T(8,128)}), f32[1,6,64,1024]{3,2,1,0:T(8,128)}) %reduce-scatter.2.cloned.1.call-update) | async-done | bytes 1572880 | tf_op jit(solution)/shard_map/reduce_scatter | solution.py:239
  982.9 40.4 %psum.7 = f32[12,1024]{1,0:T(8,128)S(1)} all-reduce(f32[12,1024]{1,0:T(8,128)S(1)} %concatenate.17), channel_id=1, replica_groups=mesh['dp'=16,'own'=2] {'dp','own'}, use_global_device_ids=true, to_apply=%region_40.41 | all-reduce | flops 12288 | bytes 98304 | tf_op jit(solution)/shard_map/psum | solution.py:213
  1032.3 96.8 %all-gather.5.cloned.1.call-done = bf16[16,6,64,1024]{3,2,1,0:T(8,128)(2,1)} async-done(((bf16[1,6,64,1024]{3,2,1,0:T(8,128)(2,1)}), bf16[16,6,64,1024]{3,2,1,0:T(8,128)(2,1)}) %all-gather.5.cloned.1.call-update) | async-done | bytes 12582928 | tf_op jit(solution)/shard_map/all_gather | solution.py:240
  1136.2 20.4 %bitcast_add_fusion.6 = f32[6,1024,1024]{2,1,0:T(8,128)} fusion(f32[16,6,64,1024]{3,2,0,1:T(8,128)S(1)} %copy_convert_fusion, f32[6,1024,1024]{2,1,0:T(8,128)} %param.24), kind=kLoop, calls=%fused_computation.273 | loop fusion | flops 12582912 | bytes 75497472 | tf_op jit(solution)/shard_map/add | solution.py:244
  1156.6 114.5 %conditional.6 = (f32[1,1024,1024]{2,1,0:T(8,128)}) conditional(s32[]{:T(128)} %bitcast.47, () %tuple.60, f32[6,1024,1024]{2,1,0:T(8,128)} %bitcast_add_fusion.6), branch_computations={%region_14.15_spmd, %region_15.17_spmd} | conditional | flops 32264683520 | bytes 117441576 | solution.py:248
  1169.4 14.0 bitcast_add_fusion
  1275.9 113.3 %conditional.11 = (f32[1,1024,1024]{2,1,0:T(8,128)}) conditional(s32[]{:T(128)} %bitcast.66, () %tuple.65, f32[6,1024,1024]{2,1,0:T(8,128)} %bitcast_add_fusion.6), branch_computations={%region_29.30_spmd, %region_30.32_spmd} | conditional | flops 32264683520 | bytes 117441576 | solution.py:248
  1309.9 14.0 multiply_add_fusion.17
  1389.2 113.6 %conditional.10 = (f32[1,1024,1024]{2,1,0:T(8,128)}) conditional(s32[]{:T(128)} %bitcast.65, () %tuple.64, f32[6,1024,1024]{2,1,0:T(8,128)} %bitcast_add_fusion.6), branch_computations={%region_26.27_spmd, %region_27.29_spmd} | conditional | flops 32264683520 | bytes 117441576 | solution.py:248
  1401.7 14.0 bitcast_add_fusion.4
  1502.8 113.4 %conditional.9 = (f32[1,1024,1024]{2,1,0:T(8,128)}) conditional(s32[]{:T(128)} %bitcast.64, () %tuple.63, f32[6,1024,1024]{2,1,0:T(8,128)} %bitcast_add_fusion.6), branch_computations={%region_23.24_spmd, %region_24.26_spmd} | conditional | flops 32264683520 | bytes 117441576 | solution.py:248
  1616.1 113.2 %conditional.8 = (f32[1,1024,1024]{2,1,0:T(8,128)}) conditional(s32[]{:T(128)} %bitcast.63, () %tuple.62, f32[6,1024,1024]{2,1,0:T(8,128)} %bitcast_add_fusion.6), branch_computations={%region_20.21_spmd, %region_21.23_spmd} | conditional | flops 32264683520 | bytes 117441576 | solution.py:248
  1729.3 113.1 %conditional.7 = (f32[1,1024,1024]{2,1,0:T(8,128)}) conditional(s32[]{:T(128)} %bitcast.62, () %tuple.61, f32[6,1024,1024]{2,1,0:T(8,128)} %bitcast_add_fusion.6), branch_computations={%region_17.18_spmd, %region_18.20_spmd} | conditional | flops 32264683520 | bytes 117441576 | solution.py:248
  1864.7 18.8 add_subtract_fusion
  (268 shorter events, 924.4 us)
Async XLA Ops:
  7.2 56.6 %all-gather.3.cloned.1.call-start = ((), (), s32[]{:S(2)}) async-start(), calls=%async_computation.1 | async-start | bytes 37748736 | tf_op jit(solution)/shard_map/all_gather | solution.py:145
  20.6 952.7 %reduce-scatter.2.cloned.1.call-start = ((), (), s32[]{:S(2)}) async-start(), calls=%async_computation.2 | async-start | bytes 51904512 | tf_op jit(solution)/shard_map/reduce_scatter | solution.py:239
  158.5 21.4 %copy-start.16 = (bf16[1,512,1,1024]{1,3,2,0:T(8,128)(2,1)}, bf16[1,512,1,1024]{1,3,2,0:T(8,128)(2,1)S(1)}, u32[]{:S(2)}) copy-start(bf16[1,512,1,1024]{1,3,2,0:T(8,128)(2,1)S(1)} %get-tuple-element.121) | copy-start | bytes 3145732
  257.6 23.1 %slice-start = ((s8[16777216]{0:T(1024)(128)(4,1)}), s8[4194304]{0:T(1024)(128)(4,1)S(1)}, s32[]{:S(2)}) async-start(s8[16777216]{0:T(1024)(128)(4,1)} %bitcast.189), calls=%async_computation.4 | async-start | bytes 8388608
  257.6 23.1 %slice-start.1 = ((s8[16777216]{0:T(1024)(128)(4,1)}), s8[4194304]{0:T(1024)(128)(4,1)S(1)}, s32[]{:S(2)}) async-start(s8[16777216]{0:T(1024)(128)(4,1)} %bitcast.189), calls=%async_computation.5 | async-start | bytes 8388608
  435.1 33.5 %copy-start.42 = (pred[2,6]{1,0:T(4,128)(4,1)S(1)}, pred[2,6]{1,0:T(4,128)(4,1)}, u32[]{:S(2)}) copy-start(pred[2,6]{1,0:T(4,128)(4,1)} %broadcast_in_dim.102) | copy-start | bytes 40
  435.1 33.5 %copy-start.43 = (pred[2,6]{1,0:T(4,128)(4,1)S(1)}, pred[2,6]{1,0:T(4,128)(4,1)}, u32[]{:S(2)}) copy-start(pred[2,6]{1,0:T(4,128)(4,1)} %compare_and_fusion) | copy-start | bytes 40
  540.4 435.4 %copy-start.51 = (pred[12]{0:T(512)(128)(4,1)S(1)}, pred[12]{0:T(512)(128)(4,1)}, u32[]{:S(2)}) copy-start(pred[12]{0:T(512)(128)(4,1)} %copy-done.50) | copy-start | bytes 40
  540.4 440.1 %copy-start.28 = (f32[4096]{0:T(1024)S(1)}, f32[4096]{0:T(1024)}, u32[]{:S(2)}) copy-start(f32[4096]{0:T(1024)} %get-tuple-element.103) | copy-start | bytes 49156
  540.4 440.2 %copy-start.7 = (bf16[16,64,512]{2,1,0:T(8,128)(2,1)S(1)}, bf16[16,64,512]{2,1,0:T(8,128)(2,1)}, u32[]{:S(2)}) copy-start(bf16[16,64,512]{2,1,0:T(8,128)(2,1)} %copy-done.6) | copy-start | bytes 3145732
  540.4 442.4 %copy-start.24 = (f32[1024]{0:T(1024)S(1)}, f32[1024]{0:T(1024)}, u32[]{:S(2)}) copy-start(f32[1024]{0:T(1024)} %get-tuple-element.96) | copy-start | bytes 12292
  540.4 442.4 %copy-start.25 = (f32[1024]{0:T(1024)S(1)}, f32[1024]{0:T(1024)}, u32[]{:S(2)}) copy-start(f32[1024]{0:T(1024)} %get-tuple-element.99) | copy-start | bytes 12292
  540.4 442.4 %copy-start.26 = (f32[1024]{0:T(1024)S(1)}, f32[1024]{0:T(1024)}, u32[]{:S(2)}) copy-start(f32[1024]{0:T(1024)} %get-tuple-element.105) | copy-start | bytes 12292
  540.4 442.4 %copy-start.27 = (f32[1024]{0:T(1024)S(1)}, f32[1024]{0:T(1024)}, u32[]{:S(2)}) copy-start(f32[1024]{0:T(1024)} %get-tuple-element.107) | copy-start | bytes 12292
  540.4 442.4 %copy-start.37 = (f32[1024]{0:T(1024)S(1)}, f32[1024]{0:T(1024)}, u32[]{:S(2)}) copy-start(f32[1024]{0:T(1024)} %get-tuple-element.94) | copy-start | bytes 12292
  540.5 442.4 %copy-start.38 = (f32[1024]{0:T(1024)S(1)}, f32[1024]{0:T(1024)}, u32[]{:S(2)}) copy-start(f32[1024]{0:T(1024)} %get-tuple-element.98) | copy-start | bytes 12292
  540.5 482.9 %copy-start.18 = (f32[12,1024]{1,0:T(8,128)S(1)}, f32[12,1024]{1,0:T(8,128)}, u32[]{:S(2)}) copy-start(f32[12,1024]{1,0:T(8,128)} %param.25) | copy-start | bytes 147460
  540.5 482.9 %copy-start.19 = (f32[12,1024]{1,0:T(8,128)S(1)}, f32[12,1024]{1,0:T(8,128)}, u32[]{:S(2)}) copy-start(f32[12,1024]{1,0:T(8,128)} %param.26) | copy-start | bytes 147460
  540.5 482.9 %copy-start.20 = (f32[12,1024]{1,0:T(8,128)S(1)}, f32[12,1024]{1,0:T(8,128)}, u32[]{:S(2)}) copy-start(f32[12,1024]{1,0:T(8,128)} %param.27) | copy-start | bytes 147460
  540.5 483.5 %copy-start.5 = (f32[512,1024]{1,0:T(8,128)S(1)}, f32[512,1024]{1,0:T(8,128)}, u32[]{:S(2)}) copy-start(f32[512,1024]{1,0:T(8,128)} %copy-done.4) | copy-start | bytes 6291460
  540.5 483.5 %copy-start.35 = (f32[512]{0:T(512)S(1)}, f32[512]{0:T(512)}, u32[]{:S(2)}) copy-start(f32[512]{0:T(512)} %copy-done.34) | copy-start | bytes 6148
  540.5 588.5 %all-gather.5.cloned.1.call-start = ((), (), s32[]{:S(2)}) async-start(), calls=%async_computation.3 | async-start | bytes 13369344 | tf_op jit(solution)/shard_map/all_gather | solution.py:240
  1842.5 18.2 copy-start.1
  1847.5 17.1 copy-start
  (40 other events, 274.1 us)
Sparse Core Ops, SparseCore 0:
  20.7 42.9 all-gather.2
  540.5 432.7 reduce-scatter.1
  976.7 152.3 all-gather.4
where the time goes:
time: 1900 us; the launch traced here: 1890 us
  matrix products  780 us (41%)
  waiting for transfers between devices  569 us (30%)
  local copies, waits for them, and re-layouts  243 us (13%)
  other arithmetic  233 us (12%)
  blocking collectives  40.4 us (2%)
    reduce_scatter x1, waiting for transfers between devices, on_device(): lax.psum_scatter(arranged, ('dp', 'own'), scatter_dimension=0, tiled=True)  433 us
    dot_general x30, matrix products, orthogonal(): jnp.dot(poly, low_iter, preferred_element_type=jnp.float32)  415 us
    dot_general x34, matrix products, contract_last(): lax.dot_general(operand_left, operand_right, (((1,), (1,)), ((), ())), pr...  267 us
    all_gather x1, waiting for transfers between devices, on_device(): lax.all_gather(share.astype(jnp.bfloat16), 'dp', axis=0, tiled=True)  96.8 us
    gather x3, local copies, waits for them, and re-layouts, on_device(): jnp.take(grad_blocks, block_index, axis=0)  71 us
    psum x1, blocking collectives, on_device(): vector_grad = lax.psum(vector_local, ('dp', 'own'))  40.4 us
    all_gather x1, waiting for transfers between devices, on_device(): lax.all_gather(matrix_master.astype(jnp.bfloat16), 'own', axis=0, tiled=T...  39.2 us
    gather x3, local copies, waits for them, and re-layouts, on_device(): blocks = jnp.take(gathered, slot_table, axis=0)  38.5 us
  transfers between devices with their start and end apart: 3, of which 3 were waited for; matrix products, arithmetic and copies ran while one was open for 1% of the time, Pallas kernels for 0%

commit v1 on v0

v1 whole, which is shorter than its diff:
```python
import math

import jax
import jax.numpy as jnp
from jax import lax
from jax.experimental import pallas as pl
from jax.experimental.pallas import tpu as pltpu
from jax.sharding import PartitionSpec as P

HEADS = 16
HEAD = 64
LEN = 512
NEWTON_STEPS = 5
STEP = 10


poly_first = 3.4445
poly_second = -4.775
poly_third = 2.0315
momentum_decay = 0.95
matrix_rate = 1.0
matrix_decay = 0.01
beta_first = 0.9
beta_second = 0.999
vector_rate = 0.2
vector_decay = 0.01
adam_epsilon = 1e-08
norm_epsilon = 1e-05
ortho_epsilon = 1e-07


def layer_norm(values, gain_row, shift_row):
    centred = values - jnp.mean(values, axis=-1, keepdims=True)
    spread = jnp.mean(centred * centred, axis=-1, keepdims=True)
    return centred * lax.rsqrt(spread + norm_epsilon) * gain_row + shift_row


def gelu_exact(values):
    return 0.5 * values * (1.0 + jax.scipy.special.erf(values * (1.0 / math.sqrt(2.0))))


def contract_last(operand_left, operand_right):
    return lax.dot_general(
        operand_left, operand_right, (((1,), (1,)), ((), ())), preferred_element_type=jnp.float32
    )


def contract_first(operand_left, operand_right):
    return lax.dot_general(
        operand_left, operand_right, (((0,), (0,)), ((), ())), preferred_element_type=jnp.float32
    )


def head_scores(queries, key_rows):
    length = queries.shape[0]
    query_heads = queries.reshape(length, HEADS, HEAD)
    key_heads = key_rows.reshape(length, HEADS, HEAD)
    scores = jnp.einsum("qhd,khd->hqk", query_heads, key_heads, preferred_element_type=jnp.float32)
    return (scores * (1.0 / math.sqrt(HEAD)), query_heads, key_heads)


def attend_forward(triple):
    queries, key_rows, values = triple
    length = queries.shape[0]
    scores, query_heads, key_heads = head_scores(queries, key_rows)
    row_peak = jnp.max(scores, axis=-1, keepdims=True)
    exps = jnp.exp(scores - row_peak)
    row_total = jnp.sum(exps, axis=-1, keepdims=True)
    probabilities = (exps / row_total).astype(jnp.bfloat16)
    value_heads = values.reshape(length, HEADS, HEAD)
    mixed = jnp.einsum(
        "hqk,khd->qhd", probabilities, value_heads, preferred_element_type=jnp.float32
    )
    return (mixed.reshape(length, HEADS * HEAD).astype(jnp.bfloat16), row_peak, row_total)


def attend_backward(bundle):
    queries, key_rows, values, grad_mixed, row_peak, row_total = bundle
    length = queries.shape[0]
    scores, query_heads, key_heads = head_scores(queries, key_rows)
    probabilities = jnp.exp(scores - row_peak) / row_total
    value_heads = values.reshape(length, HEADS, HEAD)
    grad_heads = grad_mixed.reshape(length, HEADS, HEAD)
    grad_probs = jnp.einsum(
        "qhd,khd->hqk", grad_heads, value_heads, preferred_element_type=jnp.float32
    )
    row_dot = jnp.sum(grad_probs * probabilities, axis=-1, keepdims=True)
    grad_scores = (probabilities * (grad_probs - row_dot)).astype(jnp.bfloat16)
    scale = 1.0 / math.sqrt(HEAD)
    grad_query = (
        jnp.einsum("hqk,khd->qhd", grad_scores, key_heads, preferred_element_type=jnp.float32)
        * scale
    )
    grad_key = (
        jnp.einsum("hqk,qhd->khd", grad_scores, query_heads, preferred_element_type=jnp.float32)
        * scale
    )
    grad_value = jnp.einsum(
        "hqk,qhd->khd",
        probabilities.astype(jnp.bfloat16),
        grad_heads,
        preferred_element_type=jnp.float32,
    )
    features = HEADS * HEAD
    return tuple(
        grad.reshape(length, features).astype(jnp.bfloat16)
        for grad in (grad_query, grad_key, grad_value)
    )


def newton_kernel(momentum_ref, ortho_ref, iterate, low_iter, gram, gram_low, poly):
    size = momentum_ref.shape[0]
    tile = min(512, size)
    tiles = size // tile

    def total_step(place, total):
        rows = momentum_ref[pl.ds(pl.multiple_of(place * 128, 128), 128), :]
        return total + jnp.sum(rows * rows)

    total = lax.fori_loop(0, size // 128, total_step, jnp.float32(0.0))
    norm = jnp.sqrt(jnp.full((8, 128), total, jnp.float32)) + ortho_epsilon
    inverse = (1.0 / norm)[0:1, 0:1]

    def rows_at(place):
        return pl.ds(pl.multiple_of(place * tile, tile), tile)

    @pl.loop(0, tiles)
    def _(place):
        rows = rows_at(place)
        start = momentum_ref[rows, :] * inverse
        iterate[rows, :] = start
        low_iter[rows, :] = start.astype(jnp.bfloat16)

    @pl.loop(0, NEWTON_STEPS)
    def _(sweep):
        @pl.loop(0, tiles)
        def _(place):
            rows = rows_at(place)
            product = contract_last(low_iter[rows, :], low_iter[...])
            gram[rows, :] = product
            gram_low[rows, :] = product.astype(jnp.bfloat16)

        @pl.loop(0, tiles)
        def _(place):
            rows = rows_at(place)
            square = jnp.dot(
                gram_low[rows, :], gram_low[...], preferred_element_type=jnp.float32
            )
            poly[rows, :] = (poly_second * gram[rows, :] + poly_third * square).astype(
                jnp.bfloat16
            )

        @pl.loop(0, tiles)
        def _(place):
            rows = rows_at(place)
            iterate[rows, :] = poly_first * iterate[rows, :] + jnp.dot(
                poly[rows, :], low_iter[...], preferred_element_type=jnp.float32
            )

        @pl.loop(0, tiles)
        def _(place):
            rows = rows_at(place)
            low_iter[rows, :] = iterate[rows, :].astype(jnp.bfloat16)

    ortho_ref[...] = low_iter[...]


def orthogonal(momentum):
    size = momentum.shape[0]
    return pl.pallas_call(
        newton_kernel,
        out_shape=jax.ShapeDtypeStruct((size, size), jnp.bfloat16),
        in_specs=[pl.BlockSpec(memory_space=pltpu.VMEM)],
        out_specs=pl.BlockSpec(memory_space=pltpu.VMEM),
        scratch_shapes=[
            pltpu.VMEM((size, size), jnp.float32),
            pltpu.VMEM((size, size), jnp.bfloat16),
            pltpu.VMEM((size, size), jnp.float32),
            pltpu.VMEM((size, size), jnp.bfloat16),
            pltpu.VMEM((size, size), jnp.bfloat16),
        ],
        compiler_params=pltpu.CompilerParams(vmem_limit_bytes=48 * 1024 * 1024),
        cost_estimate=pl.CostEstimate(
            flops=NEWTON_STEPS * 6 * size**3, bytes_accessed=6 * size * size, transcendentals=0
        ),
        name="newton",
    )(momentum)


def weight_grads(left, right, hidden_blocks, piece_rows):
    tokens, features = left.shape[1:]
    blocks = 4 + 2 * hidden_blocks
    half = features // 2
    group = half // piece_rows

    def left_at(block, part):
        early = jnp.where(block < 3, 0, jnp.where(block == 3, 1, 2))
        return jnp.where(block < 4 + hidden_blocks, early, block - 1 - hidden_blocks)

    def right_at(block, part):
        return jnp.minimum(block, 4 + hidden_blocks)

    def kernel(left_ref, right_ref, out_ref):
        product = contract_first(left_ref[0], right_ref[0])
        out_ref[...] = product.astype(jnp.bfloat16).reshape(group, 1, piece_rows, features)

    return pl.pallas_call(
        kernel,
        grid=(blocks, 2),
        out_shape=jax.ShapeDtypeStruct((2 * group, blocks, piece_rows, features), jnp.bfloat16),
        in_specs=[
            pl.BlockSpec((1, tokens, half), lambda b, p: (left_at(b, p), 0, p)),
            pl.BlockSpec((1, tokens, features), lambda b, p: (right_at(b, p), 0, 0)),
        ],
        out_specs=pl.BlockSpec((group, 1, piece_rows, features), lambda b, p: (p, b, 0, 0)),
        compiler_params=pltpu.CompilerParams(vmem_limit_bytes=48 * 1024 * 1024),
        cost_estimate=pl.CostEstimate(
            flops=2 * blocks * tokens * features**2,
            bytes_accessed=2 * blocks * features * (tokens + features),
            transcendentals=0,
        ),
        name="weight_grads",
    )(left, right)


def on_device(
    tokens,
    cotangent,
    slot_table,
    matrix_master,
    matrix_momentum,
    vector_params,
    vector_first,
    vector_second,
):
    features = tokens.shape[1]
    hidden_blocks = vector_params.shape[0] - 8
    slots = matrix_master.shape[0]
    owners = lax.axis_size("own")
    data_count = lax.axis_size("dp")
    slot_count = slots * owners
    f32 = jnp.float32
    gathered = lax.all_gather(matrix_master.astype(jnp.bfloat16), "own", axis=0, tiled=True)
    blocks = [
        lax.dynamic_index_in_dim(gathered, slot_table[place], 0, keepdims=False)
        for place in range(4 + 2 * hidden_blocks)
    ]
    w_query, w_key, w_value, w_out = blocks[:4]
    w_up = blocks[4 : 4 + hidden_blocks]
    w_down = blocks[4 + hidden_blocks :]

    def dot(left, right):
        return jnp.dot(left, right, preferred_element_type=f32)

    queries = (dot(tokens, w_query) + vector_params[0]).astype(jnp.bfloat16)
    key_rows = dot(tokens, w_key).astype(jnp.bfloat16)
    values = (dot(tokens, w_value) + vector_params[1]).astype(jnp.bfloat16)
    sequences = tokens.shape[0] // LEN
    triples = tuple(
        part.reshape(sequences, LEN, features) for part in (queries, key_rows, values)
    )
    mixed_rows, row_peak, row_total = lax.map(attend_forward, triples)
    mixed_rows = mixed_rows.reshape(sequences * LEN, features)
    attn_out = dot(mixed_rows, w_out) + vector_params[2]
    normed, norm_one_back = jax.vjp(
        layer_norm, tokens.astype(f32) + attn_out, vector_params[4], vector_params[5]
    )
    normed_low = normed.astype(jnp.bfloat16)
    activity, gelu_backs = [], []
    for place in range(hidden_blocks):
        full, back = jax.vjp(gelu_exact, dot(normed_low, w_up[place]) + vector_params[8 + place])
        activity.append(full.astype(jnp.bfloat16))
        gelu_backs.append(back)
    branch = vector_params[3]
    for place in range(hidden_blocks):
        branch = branch + dot(activity[place], w_down[place])
    output, norm_two_back = jax.vjp(layer_norm, normed + branch, vector_params[6], vector_params[7])
    d_resid_two, d_gain_two, d_shift_two = norm_two_back(cotangent.astype(f32))
    d_branch = d_resid_two.astype(jnp.bfloat16)
    d_hidden = [
        gelu_backs[place](contract_last(d_branch, w_down[place]))[0].astype(jnp.bfloat16)
        for place in range(hidden_blocks)
    ]
    d_normed = d_resid_two
    for place in range(hidden_blocks):
        d_normed = d_normed + contract_last(d_hidden[place], w_up[place])
    d_resid_one, d_gain_one, d_shift_one = norm_one_back(d_normed)
    d_attn = d_resid_one.astype(jnp.bfloat16)
    d_mixed = contract_last(d_attn, w_out).astype(jnp.bfloat16)
    bundle = triples + (d_mixed.reshape(sequences, LEN, features), row_peak, row_total)
    d_query, d_key, d_value = (
        part.reshape(sequences * LEN, features) for part in lax.map(attend_backward, bundle)
    )
    input_grad = (
        d_resid_one
        + contract_last(d_query, w_query)
        + contract_last(d_key, w_key)
        + contract_last(d_value, w_value)
    )
    left = jnp.stack([tokens, mixed_rows, normed_low] + activity)
    right = jnp.stack([d_query, d_key, d_value, d_attn] + d_hidden + [d_branch])
    devices = data_count * owners
    piece_rows = features // devices
    kernel_rows = max(piece_rows, 32)
    pieces = weight_grads(left, right, hidden_blocks, kernel_rows)
    if kernel_rows != piece_rows:
        finer = kernel_rows // piece_rows
        pieces = pieces.reshape(-1, pieces.shape[1], finer, piece_rows, features)
        pieces = pieces.transpose(0, 2, 1, 3, 4).reshape(devices, -1, piece_rows, features)
    share = lax.psum_scatter(pieces, ("dp", "own"), scatter_dimension=0, tiled=True)[0]

    def column_sum(part):
        return jnp.sum(part, axis=0, dtype=f32)

    vector_local = jnp.stack(
        [
            column_sum(d_query),
            column_sum(d_value),
            column_sum(d_attn),
            column_sum(d_branch),
            d_gain_one,
            d_shift_one,
            d_gain_two,
            d_shift_two,
        ]
        + [column_sum(part) for part in d_hidden]
    )
    vector_grad = jnp.sum(lax.all_gather(vector_local, ("dp", "own"), axis=0), axis=0)

    match = slot_table[None, :] == jnp.arange(slot_count, dtype=jnp.int32)[:, None]
    slot_used = jnp.any(match, axis=1)
    block_index = jnp.sum(
        jnp.where(match, jnp.arange(slot_table.shape[0], dtype=jnp.int32)[None, :], 0), axis=1
    )
    slot_share = jnp.stack(
        [lax.dynamic_index_in_dim(share, block_index[s], 0, keepdims=False) for s in range(slot_count)]
    ).reshape(owners, slots, piece_rows, features)
    mine = lax.all_to_all(slot_share, "own", split_axis=0, concat_axis=0, tiled=True)
    summed = lax.all_gather(mine, "dp", axis=0, tiled=False)
    summed = summed.transpose(2, 0, 1, 3, 4).reshape(slots, features, features).astype(f32)
    used_here = lax.dynamic_slice_in_dim(slot_used, lax.axis_index("own") * slots, slots)
    used_here = used_here[:, None, None]
    new_momentum = momentum_decay * matrix_momentum + jnp.where(used_here, summed, 0.0)

    copies = 1
    while copies * 2 * slots <= data_count:
        copies *= 2
    turn = lax.axis_index("dp")
    slot_place = jnp.minimum(turn // copies, slots - 1)
    ortho_low = orthogonal(
        lax.dynamic_index_in_dim(new_momentum, slot_place, 0, keepdims=False)
    )
    part_rows = features // copies
    ortho_part = lax.dynamic_slice_in_dim(ortho_low, (turn % copies) * part_rows, part_rows, 0)
    ortho = lax.all_gather(ortho_part, "dp", axis=0, tiled=True)[: slots * features]
    ortho = jnp.where(used_here, ortho.reshape(slots, features, features).astype(f32), 0.0)
    new_master = matrix_master - matrix_rate * (ortho + matrix_decay * matrix_master)
    new_first = beta_first * vector_first + (1.0 - beta_first) * vector_grad
    new_second = beta_second * vector_second + (1.0 - beta_second) * vector_grad * vector_grad
    first_hat = new_first / (1.0 - beta_first**STEP)
    second_hat = new_second / (1.0 - beta_second**STEP)
    new_params = vector_params - vector_rate * (
        first_hat / (jnp.sqrt(second_hat) + adam_epsilon) + vector_decay * vector_params
    )
    return (output, input_grad, new_master, new_momentum, new_params, new_first, new_second)


def solution(mesh):
    in_specs = (
        P(("dp", "own"), None),
        P(("dp", "own"), None),
        P(),
        P("own", None, None),
        P("own", None, None),
        P(),
        P(),
        P(),
    )
    out_specs = (
        P(("dp", "own"), None),
        P(("dp", "own"), None),
        P("own", None, None),
        P("own", None, None),
        P(),
        P(),
        P(),
    )
    return jax.shard_map(
        on_device, mesh=mesh, in_specs=in_specs, out_specs=out_specs, check_vma=False
    )
```

time: 1900 us -> 979 us (0.52)
  matrix products: 780 us -> 121 us
  local copies, waits for them, and re-layouts: 243 us -> 65.9 us
  other arithmetic: 233 us -> 73.7 us
  Pallas kernels: 0 us -> 75.9 us
  between operations: 18.7 us -> 60.9 us
  blocking collectives: 40.4 us -> 5.12 us
    dot_general x38 -> x12, matrix products: 468 us -> 39.5 us  [dot(): return jnp.dot(left, right, preferred_element_type=f32)]
    dot_general x34 -> x12, matrix products: 267 us -> 36.4 us  [contract_last(): lax.dot_general(operand_left, operand_right, (((1,), (1,)), ((), ())), pr...]
    all_gather x1 -> x3, waiting for transfers between devices: 96.8 us -> 327 us  [the longest x1 177 us: on_device(): lax.all_gather(ortho_part, 'dp', axis=0, tiled=True)[:slots * features]]
    reduce_scatter x1, waiting for transfers between devices: 433 us -> 222 us  [on_device(): lax.psum_scatter(pieces, ('dp', 'own'), scatter_dimension=0, tiled=True)[0]]
    gather x6 -> x0, local copies, waits for them, and re-layouts: 110 us -> none  [the longest x3 71 us: on_device(): jnp.take(grad_blocks, block_index, axis=0)]
    pallas_call x0 -> x2, Pallas kernels: none -> 75.9 us  [the longest x1 43.9 us: orthogonal(): pl.pallas_call(newton_kernel, out_shape=jax.ShapeDtypeStruct((size, size)...]
    transpose x4 -> x0, local copies, waits for them, and re-layouts: 61.8 us -> none  [the longest x1 34.9 us: on_device(): slot_grad.reshape(owners, slots, data_count, piece_rows, features)]
    psum x1 -> x0, blocking collectives: 40.4 us -> none  [on_device(): vector_grad = lax.psum(vector_local, ('dp', 'own'))]
  transfers between devices with their start and end apart: 3 -> 5, of which waited for: 3 -> 4; matrix products, arithmetic and copies ran while one was open for 1% -> 6% of each run, Pallas kernels for 0% -> 5%
where the time goes in v1:
time: 979 us; the launch traced here: 970 us
  waiting for transfers between devices  567 us (58%)
  matrix products  121 us (12%)
  Pallas kernels  75.9 us (8%)
  other arithmetic  73.7 us (8%)
  local copies, waits for them, and re-layouts  65.9 us (7%)
  between operations  60.9 us (6%)
    reduce_scatter x1, waiting for transfers between devices, on_device(): lax.psum_scatter(pieces, ('dp', 'own'), scatter_dimension=0, tiled=True)[0]  222 us
    all_gather x1, waiting for transfers between devices, on_device(): lax.all_gather(ortho_part, 'dp', axis=0, tiled=True)[:slots * features]  177 us
    all_gather x1, waiting for transfers between devices, on_device(): summed = lax.all_gather(mine, 'dp', axis=0, tiled=False)  150 us
    pallas_call x1, Pallas kernels, orthogonal(): pl.pallas_call(newton_kernel, out_shape=jax.ShapeDtypeStruct((size, size)...  43.9 us
    dot_general x12, matrix products, dot(): return jnp.dot(left, right, preferred_element_type=f32)  39.5 us
    unnamed x109, local copies, waits for them, and re-layouts  38.5 us
    dot_general x12, matrix products, contract_last(): lax.dot_general(operand_left, operand_right, (((1,), (1,)), ((), ())), pr...  36.4 us
    pallas_call x1, Pallas kernels, weight_grads(): pl.pallas_call(kernel, grid=(blocks, 2), out_shape=jax.ShapeDtypeStruct((...  32 us
  transfers between devices with their start and end apart: 5, of which 4 were waited for; matrix products, arithmetic and copies ran while one was open for 6% of the time, Pallas kernels for 5%

profile of v1, /device:TPU:0, one launch (start us, length us, event | category | flops | bytes accessed | tf_op | source)
XLA Modules:
  0.0 970.0 jit_solution(13317439900015580670)
XLA Ops:
  7.2 13.3 %convert_element_type.203 = bf16[6,1024,1024]{2,1,0:T(8,128)(2,1)} convert(f32[6,1024,1024]{2,1,0:T(8,128)} %param.11) | non-fusion elementwise | flops 6291456 | bytes 37748736 | tf_op jit(solution)/shard_map/convert_element_type | solution.py:243
  45.9 17.8 %all-gather.8.cloned.1.call-done = bf16[12,1024,1024]{2,1,0:T(8,128)(2,1)} async-done(((bf16[6,1024,1024]{2,1,0:T(8,128)(2,1)}), bf16[12,1024,1024]{2,1,0:T(8,128)(2,1)}) %all-gather.8.cloned.1.call-update) | async-done | bytes 25165840 | tf_op jit(solution)/shard_map/all_gather | solution.py:243
  69.9 9.1 fusion.159
  81.9 7.7 fusion.97
  96.7 4.2 bitcast_dynamic-update-slice_fusion.9
  100.9 4.9 bitcast_dynamic-update-slice_fusion.8
  105.7 4.8 bitcast_dynamic-update-slice_fusion.7
  110.5 4.8 bitcast_dynamic-update-slice_fusion.6
  159.8 13.7 %multiply_reduce_fusion = (f32[16,512]{1,0:T(8,128)S(1)}, f32[16,512,512]{1,2,0:T(8,128)}) fusion(f32[16,512,512]{1,2,0:T(8,128)} %get-tuple-element.121, f32[16,512]{1,0:T(8,128)S(1)} %get-tuple-element.120, bf16[512,16,64]{0,2,1:T(8,128)(2,1)} %bitcast.295, bf16[512,16,64]{0,2,1:T(8,128)(2,1)} %bitcast.336), kind=kOutput, calls=%fused_computation.8 | convolution fusion | flops 549445632 | bytes 35717120 | tf_op jit(solution)/shard_map/while/body/eval_jaxpr/qhd,khd->hqk/dot_general | solution.py:84
  176.9 8.1 multiply_convert_fusion
  190.4 9.4 convert_reduce_fusion.7
  214.1 32.0 %weight_grads.1 = bf16[32,12,32,1024]{3,2,1,0:T(8,128)(2,1)} custom-call(bf16[7,512,1024]{2,1,0:T(8,128)(2,1)} %get-tuple-element.71.left_ref, bf16[9,512,1024]{2,1,0:T(8,128)(2,1)} %bitcast_dynamic-update-slice_fusion.right_ref), custom_call_target="tpu_custom_call" | custom-call | flops 12884901888 | bytes 37748736 | tf_op jit(solution)/shard_map/weight_grads/pallas_call | solution.py:207
  270.7 222.1 %reduce-scatter.2.cloned.1.call-done = bf16[1,12,32,1024]{3,2,1,0:T(8,128)(2,1)} async-done(((bf16[32,12,32,1024]{3,2,1,0:T(8,128)(2,1)}), bf16[1,12,32,1024]{3,2,1,0:T(8,128)(2,1)}) %reduce-scatter.2.cloned.1.call-update) | async-done | bytes 786448 | tf_op jit(solution)/shard_map/reduce_scatter | solution.py:310
  503.0 5.1 all_to_all.5
  510.0 150.0 %all-gather.12.cloned.1.call-done = bf16[32,6,32,1024]{3,2,1,0:T(8,128)(2,1)} async-done(((bf16[2,6,32,1024]{3,2,1,0:T(8,128)(2,1)}), bf16[32,6,32,1024]{3,2,1,0:T(8,128)(2,1)}) %all-gather.12.cloned.1.call-update) | async-done | bytes 12582928 | tf_op jit(solution)/shard_map/all_gather | solution.py:339
  659.9 7.2 convert_bitcast_fusion
  667.1 8.8 copy.54
  675.8 16.7 %fusion.3 = f32[6,1024,1024]{2,1,0:T(8,128)S(1)} fusion(f32[6,16,2,32,1024]{4,3,2,1,0:T(8,128)} %copy.54, f32[6,1024,1024]{2,1,0:T(8,128)} %param.12, pred[6]{0:T(512)(128)(4,1)S(1)} %dynamic_slice.140), kind=kLoop, calls=%fused_computation.6 | loop fusion | flops 18874368 | bytes 75497480 | tf_op jit(solution)/shard_map/add | solution.py:343
  692.6 8.9 copy-done
  703.8 43.9 %newton.1 = bf16[1024,1024]{1,0:T(8,128)(2,1)S(1)} custom-call(f32[1024,1024]{1,0:T(8,128)} %dynamic-slice_bitcast_fusion.momentum_ref), custom_call_target="tpu_custom_call" | custom-call | flops 32212254720 | bytes 6291456 | tf_op jit(solution)/shard_map/newton/pallas_call | solution.py:170
  754.8 4.8 add_add_fusion.2
  762.2 176.9 %all-gather.10.cloned.1.call-done = bf16[8192,1024]{1,0:T(8,128)(2,1)} async-done(((bf16[512,1024]{1,0:T(8,128)(2,1)}), bf16[8192,1024]{1,0:T(8,128)(2,1)}) %all-gather.10.cloned.1.call-update) | async-done | bytes 16777232 | tf_op jit(solution)/shard_map/all_gather | solution.py:355
  939.1 4.6 slice-done
  943.6 19.3 %fusion.2 = f32[6,1024,1024]{2,1,0:T(8,128)} fusion(f32[6,1024,1024]{2,1,0:T(8,128)} %param.11, bf16[6,1024,1024]{2,1,0:T(8,128)(2,1)S(1)} %bitcast.281, pred[6]{0:T(512)(128)(4,1)S(1)} %dynamic_slice.140), kind=kLoop, calls=%fused_computation.3 | loop fusion | flops 31457280 | bytes 62914568 | tf_op jit(solution)/shard_map/sub | solution.py:357
  (179 shorter events, 110.9 us)
Async XLA Ops:
  7.2 56.6 %all-gather.8.cloned.1.call-start = ((), (), s32[]{:S(2)}) async-start(), calls=%async_computation.2 | async-start | bytes 37748736 | tf_op jit(solution)/shard_map/all_gather | solution.py:243
  20.6 24.2 %copy-start.22 = (f32[12,1024]{1,0:T(8,128)S(1)}, f32[12,1024]{1,0:T(8,128)}, u32[]{:S(2)}) copy-start(f32[12,1024]{1,0:T(8,128)} %param.13) | copy-start | bytes 147460
  20.6 24.2 %copy-start.13 = (bf16[512,1024]{1,0:T(8,128)(2,1)S(1)}, bf16[512,1024]{1,0:T(8,128)(2,1)}, u32[]{:S(2)}) copy-start(bf16[512,1024]{1,0:T(8,128)(2,1)} %param.8) | copy-start | bytes 3145732
  20.6 472.3 %reduce-scatter.2.cloned.1.call-start = ((), (), s32[]{:S(2)}) async-start(), calls=%async_computation.3 | async-start | bytes 25952256 | tf_op jit(solution)/shard_map/reduce_scatter | solution.py:310
  69.9 9.1 copy-start.12
  81.9 7.8 copy-start.30
  90.7 24.6 %slice-start.5 = ((s8[25165824]{0:T(1024)(128)(4,1)}), s8[4194304]{0:T(1024)(128)(4,1)S(1)}, s32[]{:S(2)}) async-start(s8[25165824]{0:T(1024)(128)(4,1)} %bitcast.301), calls=%async_computation.12 | async-start | bytes 8388608
  90.7 24.6 %slice-start.6 = ((s8[25165824]{0:T(1024)(128)(4,1)}), s8[4194304]{0:T(1024)(128)(4,1)S(1)}, s32[]{:S(2)}) async-start(s8[25165824]{0:T(1024)(128)(4,1)} %bitcast.301), calls=%async_computation.13 | async-start | bytes 8388608
  96.7 18.6 %slice-start.7 = ((s8[25165824]{0:T(1024)(128)(4,1)}), s8[4194304]{0:T(1024)(128)(4,1)S(1)}, s32[]{:S(2)}) async-start(s8[25165824]{0:T(1024)(128)(4,1)} %bitcast.301), calls=%async_computation.14 | async-start | bytes 8388608
  100.9 14.4 %slice-start.8 = ((s8[25165824]{0:T(1024)(128)(4,1)}), s8[4194304]{0:T(1024)(128)(4,1)S(1)}, s32[]{:S(2)}) async-start(s8[25165824]{0:T(1024)(128)(4,1)} %bitcast.301), calls=%async_computation.15 | async-start | bytes 8388608
  105.7 9.6 slice-start.9
  110.5 4.8 slice-start.10
  128.6 12.3 %copy-start.6 = (bf16[512,1024]{1,0:T(8,128)(2,1)}, bf16[512,1024]{1,0:T(8,128)(2,1)S(1)}, u32[]{:S(2)}) copy-start(bf16[512,1024]{1,0:T(8,128)(2,1)S(1)} %get-tuple-element.68) | copy-start | bytes 3145732
  130.9 17.5 %copy-start.3 = (bf16[512,1024]{1,0:T(8,128)(2,1)}, bf16[512,1024]{1,0:T(8,128)(2,1)S(1)}, u32[]{:S(2)}) copy-start(bf16[512,1024]{1,0:T(8,128)(2,1)S(1)} %get-tuple-element.139) | copy-start | bytes 3145732
  153.0 5.5 copy-start.28
  159.8 13.7 %slice-start.1 = ((s8[16777216]{0:T(1024)(128)(4,1)}), s8[4194304]{0:T(1024)(128)(4,1)S(1)}, s32[]{:S(2)}) async-start(s8[16777216]{0:T(1024)(128)(4,1)} %bitcast.282), calls=%async_computation.8 | async-start | bytes 8388608
  159.8 14.5 %slice-start.2 = ((s8[16777216]{0:T(1024)(128)(4,1)}), s8[4194304]{0:T(1024)(128)(4,1)S(1)}, s32[]{:S(2)}) async-start(s8[16777216]{0:T(1024)(128)(4,1)} %bitcast.282), calls=%async_computation.9 | async-start | bytes 8388608
  159.8 15.8 %slice-start.3 = ((s8[16777216]{0:T(1024)(128)(4,1)}), s8[4194304]{0:T(1024)(128)(4,1)S(1)}, s32[]{:S(2)}) async-start(s8[16777216]{0:T(1024)(128)(4,1)} %bitcast.282), calls=%async_computation.10 | async-start | bytes 8388608
  159.8 17.0 %slice-start.4 = ((s8[16777216]{0:T(1024)(128)(4,1)}), s8[4194304]{0:T(1024)(128)(4,1)S(1)}, s32[]{:S(2)}) async-start(s8[16777216]{0:T(1024)(128)(4,1)} %bitcast.282), calls=%async_computation.11 | async-start | bytes 8388608
  246.1 413.8 %all-gather.12.cloned.1.call-start = ((), (), s32[]{:S(2)}) async-start(), calls=%async_computation.5 | async-start | bytes 13369344 | tf_op jit(solution)/shard_map/all_gather | solution.py:339
  508.1 251.5 %all-gather.14.cloned.1.call-start = ((), (), s32[]{:S(2)}) async-start(), calls=%async_computation.6 | async-start | bytes 2162688 | tf_op jit(solution)/shard_map/all_gather | solution.py:328
  509.9 429.2 %all-gather.10.cloned.1.call-start = ((), (), s32[]{:S(2)}) async-start(), calls=%async_computation.4 | async-start | bytes 17825792 | tf_op jit(solution)/shard_map/all_gather | solution.py:355
  692.6 8.9 copy-start
  939.1 4.6 slice-start
  (26 other events, 57.7 us)
Sparse Core Ops, SparseCore 0:
  20.7 42.9 all-gather.7
  246.2 246.5 reduce-scatter.1
  508.3 151.6 all-gather.11
  663.6 54.5 all-gather.13
  748.9 190.0 all-gather.9

commit v2 on v1

--- a/solution.py
+++ b/solution.py
@@ -187,18 +187,10 @@
     )(momentum)
 
 
-def weight_grads(left, right, hidden_blocks, piece_rows):
+def weight_grads(left, right, left_at, right_at, blocks, piece_rows):
     tokens, features = left.shape[1:]
-    blocks = 4 + 2 * hidden_blocks
     half = features // 2
     group = half // piece_rows
-
-    def left_at(block, part):
-        early = jnp.where(block < 3, 0, jnp.where(block == 3, 1, 2))
-        return jnp.where(block < 4 + hidden_blocks, early, block - 1 - hidden_blocks)
-
-    def right_at(block, part):
-        return jnp.minimum(block, 4 + hidden_blocks)
 
     def kernel(left_ref, right_ref, out_ref):
         product = contract_first(left_ref[0], right_ref[0])
@@ -209,8 +201,8 @@
         grid=(blocks, 2),
         out_shape=jax.ShapeDtypeStruct((2 * group, blocks, piece_rows, features), jnp.bfloat16),
         in_specs=[
-            pl.BlockSpec((1, tokens, half), lambda b, p: (left_at(b, p), 0, p)),
-            pl.BlockSpec((1, tokens, features), lambda b, p: (right_at(b, p), 0, 0)),
+            pl.BlockSpec((1, tokens, half), lambda b, p: (left_at(b), 0, p)),
+            pl.BlockSpec((1, tokens, features), lambda b, p: (right_at(b), 0, 0)),
         ],
         out_specs=pl.BlockSpec((group, 1, piece_rows, features), lambda b, p: (p, b, 0, 0)),
         compiler_params=pltpu.CompilerParams(vmem_limit_bytes=48 * 1024 * 1024),
@@ -221,6 +213,25 @@
         ),
         name="weight_grads",
     )(left, right)
+
+
+def chip_sum(pieces, piece_rows):
+    owners = lax.axis_size("own")
+    kernel_rows = pieces.shape[2]
+    if kernel_rows != piece_rows:
+        finer = kernel_rows // piece_rows
+        pieces = pieces.reshape(pieces.shape[0], -1, finer, piece_rows, pieces.shape[3])
+        pieces = pieces.transpose(0, 2, 1, 3, 4).reshape(
+            pieces.shape[0] * finer, -1, piece_rows, pieces.shape[4]
+        )
+    if owners != 2:
+        return lax.psum_scatter(pieces, "own", scatter_dimension=0, tiled=True)
+    halves = pieces.reshape((owners, -1) + pieces.shape[1:])
+    me = lax.axis_index("own")
+    kept = lax.dynamic_index_in_dim(halves, me, 0, keepdims=False)
+    sent = lax.dynamic_index_in_dim(halves, 1 - me, 0, keepdims=False)
+    got = lax.ppermute(sent, "own", [(0, 1), (1, 0)])
+    return (kept.astype(jnp.float32) + got.astype(jnp.float32)).astype(jnp.bfloat16)
 
 
 def on_device(
@@ -286,29 +297,45 @@
         d_normed = d_normed + contract_last(d_hidden[place], w_up[place])
     d_resid_one, d_gain_one, d_shift_one = norm_one_back(d_normed)
     d_attn = d_resid_one.astype(jnp.bfloat16)
+    devices = data_count * owners
+    piece_rows = features // devices
+    kernel_rows = max(piece_rows, 32)
+    feed_pieces = weight_grads(
+        jnp.stack([normed_low] + activity),
+        jnp.stack(d_hidden + [d_branch]),
+        lambda place: jnp.maximum(place + 1 - hidden_blocks, 0),
+        lambda place: jnp.minimum(place, hidden_blocks),
+        2 * hidden_blocks,
+        kernel_rows,
+    )
+    d_attn, feed_pieces = lax.optimization_barrier((d_attn, feed_pieces))
+    feed_sum = chip_sum(feed_pieces, piece_rows)
+    feed_share = lax.psum_scatter(feed_sum, "dp", scatter_dimension=0, tiled=True)[0]
     d_mixed = contract_last(d_attn, w_out).astype(jnp.bfloat16)
     bundle = triples + (d_mixed.reshape(sequences, LEN, features), row_peak, row_total)
     d_query, d_key, d_value = (
         part.reshape(sequences * LEN, features) for part in lax.map(attend_backward, bundle)
     )
+    d_query, d_key, d_value, feed_sum = lax.optimization_barrier(
+        (d_query, d_key, d_value, feed_sum)
+    )
+    attn_pieces = weight_grads(
+        jnp.stack([tokens, mixed_rows]),
+        jnp.stack([d_query, d_key, d_value, d_attn]),
+        lambda place: place // 3,
+        lambda place: place,
+        4,
+        kernel_rows,
+    )
+    attn_sum = chip_sum(attn_pieces, piece_rows)
+    attn_share = lax.psum_scatter(attn_sum, "dp", scatter_dimension=0, tiled=True)[0]
+    share = jnp.concatenate([attn_share, feed_share], axis=0)
     input_grad = (
         d_resid_one
         + contract_last(d_query, w_query)
         + contract_last(d_key, w_key)
         + contract_last(d_value, w_value)
     )
-    left = jnp.stack([tokens, mixed_rows, normed_low] + activity)
-    right = jnp.stack([d_query, d_key, d_value, d_attn] + d_hidden + [d_branch])
-    devices = data_count * owners
-    piece_rows = features // devices
-    kernel_rows = max(piece_rows, 32)
-    pieces = weight_grads(left, right, hidden_blocks, kernel_rows)
-    if kernel_rows != piece_rows:
-        finer = kernel_rows // piece_rows
-        pieces = pieces.reshape(-1, pieces.shape[1], finer, piece_rows, features)
-        pieces = pieces.transpose(0, 2, 1, 3, 4).reshape(devices, -1, piece_rows, features)
-    share = lax.psum_scatter(pieces, ("dp", "own"), scatter_dimension=0, tiled=True)[0]
-
     def column_sum(part):
         return jnp.sum(part, axis=0, dtype=f32)
 
@@ -325,7 +352,7 @@
         ]
         + [column_sum(part) for part in d_hidden]
     )
-    vector_grad = jnp.sum(lax.all_gather(vector_local, ("dp", "own"), axis=0), axis=0)
+    vector_chip = lax.psum(vector_local, "own").astype(jnp.bfloat16)
 
     match = slot_table[None, :] == jnp.arange(slot_count, dtype=jnp.int32)[:, None]
     slot_used = jnp.any(match, axis=1)
@@ -336,8 +363,23 @@
         [lax.dynamic_index_in_dim(share, block_index[s], 0, keepdims=False) for s in range(slot_count)]
     ).reshape(owners, slots, piece_rows, features)
     mine = lax.all_to_all(slot_share, "own", split_axis=0, concat_axis=0, tiled=True)
-    summed = lax.all_gather(mine, "dp", axis=0, tiled=False)
-    summed = summed.transpose(2, 0, 1, 3, 4).reshape(slots, features, features).astype(f32)
+    rows_here = owners * slots * piece_rows
+    vector_rows = vector_chip.shape[0]
+    padded = -(-(rows_here + vector_rows) // 16) * 16
+    outgoing = jnp.concatenate(
+        [
+            mine.reshape(rows_here, features),
+            vector_chip,
+            jnp.zeros((padded - rows_here - vector_rows, features), jnp.bfloat16),
+        ],
+        axis=0,
+    )
+    incoming = lax.all_gather(outgoing, "dp", axis=0, tiled=False)
+    vector_grad = jnp.sum(
+        incoming[:, rows_here : rows_here + vector_rows].astype(f32), axis=0
+    )
+    summed = incoming[:, :rows_here].reshape(data_count, owners, slots, piece_rows, features)
+    summed = summed.transpose(2, 1, 0, 3, 4).reshape(slots, features, features).astype(f32)
     used_here = lax.dynamic_slice_in_dim(slot_used, lax.axis_index("own") * slots, slots)
     used_here = used_here[:, None, None]
     new_momentum = momentum_decay * matrix_momentum + jnp.where(used_here, summed, 0.0)
@@ -346,10 +388,13 @@
     while copies * 2 * slots <= data_count:
         copies *= 2
     turn = lax.axis_index("dp")
+    place_of = [min(index // copies, slots - 1) for index in range(data_count)]
+    by_turn = jnp.stack([mine[:, place] for place in place_of])
+    my_rows = lax.all_to_all(by_turn, "dp", split_axis=0, concat_axis=0, tiled=True)
+    my_summed = my_rows.transpose(1, 0, 2, 3).reshape(features, features).astype(f32)
     slot_place = jnp.minimum(turn // copies, slots - 1)
-    ortho_low = orthogonal(
-        lax.dynamic_index_in_dim(new_momentum, slot_place, 0, keepdims=False)
-    )
+    my_momentum = lax.dynamic_index_in_dim(matrix_momentum, slot_place, 0, keepdims=False)
+    ortho_low = orthogonal(momentum_decay * my_momentum + my_summed)
     part_rows = features // copies
     ortho_part = lax.dynamic_slice_in_dim(ortho_low, (turn % copies) * part_rows, part_rows, 0)
     ortho = lax.all_gather(ortho_part, "dp", axis=0, tiled=True)[: slots * features]

time: 979 us -> 1020 us (1.042)
  other arithmetic: 73.7 us -> 112 us
    all_gather x2 -> x1, waiting for transfers between devices: 150 us -> 45.1 us  [on_device(): incoming = lax.all_gather(outgoing, 'dp', axis=0, tiled=False)]
    all_to_all x0 -> x1, waiting for transfers between devices: none -> 70.8 us  [on_device(): lax.all_to_all(by_turn, 'dp', split_axis=0, concat_axis=0, tiled=True)]
    add x1, other arithmetic: 16.7 us -> 44.6 us  [on_device(): momentum_decay * matrix_momentum + jnp.where(used_here, summed, 0.0)]
    reduce_scatter x1 -> x2, waiting for transfers between devices: 222 us -> 245 us  [the longest x1 180 us: on_device(): lax.psum_scatter(feed_sum, 'dp', scatter_dimension=0, tiled=True)[0]]
    unnamed x109 -> x87, local copies, waits for them, and re-layouts: 38.5 us -> 16 us
    sub x1 -> x0, other arithmetic: 19.3 us -> none  [on_device(): matrix_master - matrix_rate * (ortho + matrix_decay * matrix_master)]
    pallas_call x1 -> x2, Pallas kernels: 32 us -> 29.9 us  [weight_grads(): pl.pallas_call(kernel, grid=(blocks, 2), out_shape=jax.ShapeDtypeStruct((...]
  transfers between devices with their start and end apart: 5 -> 8, of which waited for: 4 -> 7; matrix products, arithmetic and copies ran while one was open for 6% -> 9% of each run, Pallas kernels for 5% -> 4%
where the time goes in v2:
time: 1020 us; the launch traced here: 1010 us
  waiting for transfers between devices  561 us (55%)
  matrix products  122 us (12%)
  other arithmetic  112 us (11%)
  Pallas kernels  74.1 us (7%)
  local copies, waits for them, and re-layouts  64.6 us (6%)
  between operations  59.9 us (6%)
    reduce_scatter x1, waiting for transfers between devices, on_device(): lax.psum_scatter(feed_sum, 'dp', scatter_dimension=0, tiled=True)[0]  180 us
    all_gather x1, waiting for transfers between devices, on_device(): lax.all_gather(ortho_part, 'dp', axis=0, tiled=True)[:slots * features]  173 us
    all_to_all x1, waiting for transfers between devices, on_device(): lax.all_to_all(by_turn, 'dp', split_axis=0, concat_axis=0, tiled=True)  70.8 us
    reduce_scatter x1, waiting for transfers between devices, on_device(): lax.psum_scatter(attn_sum, 'dp', scatter_dimension=0, tiled=True)[0]  65 us
    all_gather x1, waiting for transfers between devices, on_device(): incoming = lax.all_gather(outgoing, 'dp', axis=0, tiled=False)  45.1 us
    add x1, other arithmetic, on_device(): momentum_decay * matrix_momentum + jnp.where(used_here, summed, 0.0)  44.6 us
    pallas_call x1, Pallas kernels, orthogonal(): pl.pallas_call(newton_kernel, out_shape=jax.ShapeDtypeStruct((size, size)...  44.2 us
    dot_general x12, matrix products, contract_last(): lax.dot_general(operand_left, operand_right, (((1,), (1,)), ((), ())), pr...  44 us
  transfers between devices with their start and end apart: 8, of which 7 were waited for; matrix products, arithmetic and copies ran while one was open for 9% of the time, Pallas kernels for 4%

profile of v2, /device:TPU:0, one launch (start us, length us, event | category | flops | bytes accessed | tf_op | source)
XLA Modules:
  0.0 1010.3 jit_solution(4074395702556273825)
XLA Ops:
  7.2 13.3 %convert_element_type.210 = bf16[6,1024,1024]{2,1,0:T(8,128)(2,1)} convert(f32[6,1024,1024]{2,1,0:T(8,128)} %param.11) | non-fusion elementwise | flops 6291456 | bytes 37748736 | tf_op jit(solution)/shard_map/convert_element_type | solution.py:254
  44.7 19.1 %all-gather.5.cloned.1.call-done = bf16[12,1024,1024]{2,1,0:T(8,128)(2,1)} async-done(((bf16[6,1024,1024]{2,1,0:T(8,128)(2,1)}), bf16[12,1024,1024]{2,1,0:T(8,128)(2,1)}) %all-gather.5.cloned.1.call-update) | async-done | bytes 25165840 | tf_op jit(solution)/shard_map/all_gather | solution.py:254
  69.9 9.1 fusion.183
  83.0 7.4 fusion.99
  157.5 18.9 %weight_grads.2 = bf16[32,8,32,1024]{3,2,1,0:T(8,128)(2,1)} custom-call(bf16[5,512,1024]{2,1,0:T(8,128)(2,1)S(1)} %get-tuple-element.79.left_ref, bf16[5,512,1024]{2,1,0:T(8,128)(2,1)} %copy-done.33), custom_call_target="tpu_custom_call" | custom-call | flops 8589934592 | bytes 25165824 | tf_op jit(solution)/shard_map/weight_grads/pallas_call | solution.py:199
  180.7 8.5 dynamic-slice_bitcast_fusion
  190.9 10.9 %multiply_reduce_fusion = (f32[16,512]{1,0:T(8,128)S(1)}, f32[16,512,512]{1,2,0:T(8,128)}) fusion(f32[16,512,512]{1,2,0:T(8,128)} %get-tuple-element.131, f32[16,512]{1,0:T(8,128)S(1)} %get-tuple-element.130, bf16[512,16,64]{0,2,1:T(8,128)(2,1)S(1)} %bitcast.374, bf16[512,16,64]{0,2,1:T(8,128)(2,1)S(1)} %bitcast.415), kind=kOutput, calls=%fused_computation.10 | convolution fusion | flops 549445632 | bytes 35717120 | tf_op jit(solution)/shard_map/while/body/eval_jaxpr/qhd,khd->hqk/dot_general | solution.py:84
  201.9 11.7 %multiply_convert_fusion = bf16[16,512,512]{1,2,0:T(8,128)(2,1)S(1)} fusion(f32[16,512,512]{1,2,0:T(8,128)} %get-tuple-element.151, f32[16,512]{1,0:T(8,128)S(1)} %get-tuple-element.150, f32[16,512,512]{1,2,0:T(8,128)} %get-tuple-element.131, f32[16,512]{1,0:T(8,128)S(1)} %get-tuple-element.130), kind=kLoop, calls=%fused_computation.9 | loop fusion | flops 16777216 | bytes 42008576 | tf_op jit(solution)/shard_map/while/body/eval_jaxpr/convert_element_type | solution.py:88
  218.6 9.4 fusion.102
  228.1 9.0 fusion.4
  246.7 11.0 %weight_grads.3 = bf16[32,4,32,1024]{3,2,1,0:T(8,128)(2,1)} custom-call(bf16[2,512,1024]{2,1,0:T(8,128)(2,1)S(1)} %pad_maximum_fusion.1.left_ref, bf16[4,512,1024]{2,1,0:T(8,128)(2,1)} %pad_maximum_fusion.right_ref), custom_call_target="tpu_custom_call" | custom-call | flops 4294967296 | bytes 12582912 | tf_op jit(solution)/shard_map/weight_grads/pallas_call | solution.py:199
  261.0 6.9 collective-permute-done.1
  303.8 65.0 %reduce-scatter.3.cloned.1.call-done = bf16[1,4,32,1024]{3,2,1,0:T(8,128)(2,1)} async-done(((bf16[16,4,32,1024]{3,2,1,0:T(8,128)(2,1)}), bf16[1,4,32,1024]{3,2,1,0:T(8,128)(2,1)}) %reduce-scatter.3.cloned.1.call-update) | async-done | bytes 262160 | tf_op jit(solution)/shard_map/reduce_scatter | solution.py:331
  368.8 180.3 %reduce-scatter.5.cloned.1.call-done = bf16[1,8,32,1024]{3,2,1,0:T(8,128)(2,1)} async-done(((bf16[16,8,32,1024]{3,2,1,0:T(8,128)(2,1)}), bf16[1,8,32,1024]{3,2,1,0:T(8,128)(2,1)}) %reduce-scatter.5.cloned.1.call-update) | async-done | bytes 524304 | tf_op jit(solution)/shard_map/reduce_scatter | solution.py:313
  568.4 8.0 all-to-all-start.1
  576.5 70.8 %all-to-all-done.1 = bf16[16,2,32,1024]{3,2,1,0:T(8,128)(2,1)S(1)} async-done(((bf16[16,2,32,1024]{3,2,1,0:T(8,128)(2,1)}), bf16[16,2,32,1024]{3,2,1,0:T(8,128)(2,1)S(1)}, u32[]{:S(2)}, u32[]{:S(2)}) %all-to-all-start.1) | async-done | bytes 2097184 | tf_op jit(solution)/shard_map/all_to_all | solution.py:393
  648.1 5.6 bitcast_add_fusion.momentum_ref
  653.7 44.2 %newton.1 = bf16[1024,1024]{1,0:T(8,128)(2,1)S(1)} custom-call(f32[1024,1024]{1,0:T(8,128)} %bitcast_add_fusion.momentum_ref), custom_call_target="tpu_custom_call" | custom-call | flops 32212254720 | bytes 6291456 | tf_op jit(solution)/shard_map/newton/pallas_call | solution.py:170
  710.1 45.1 %all-gather.9.cloned.1.call-done = bf16[6400,1024]{1,0:T(8,128)(2,1)} async-done(((bf16[400,1024]{1,0:T(8,128)(2,1)}), bf16[6400,1024]{1,0:T(8,128)(2,1)}) %all-gather.9.cloned.1.call-update) | async-done | bytes 13107216 | tf_op jit(solution)/shard_map/all_gather | solution.py:377
  755.2 6.2 slice.197
  764.6 8.6 copy.97
  775.1 173.1 %all-gather.7.cloned.1.call-done = bf16[8192,1024]{1,0:T(8,128)(2,1)} async-done(((bf16[512,1024]{1,0:T(8,128)(2,1)}), bf16[8192,1024]{1,0:T(8,128)(2,1)}) %all-gather.7.cloned.1.call-update) | async-done | bytes 16777232 | tf_op jit(solution)/shard_map/all_gather | solution.py:400
  948.2 10.6 %slice.196 = bf16[6144,1024]{1,0:T(8,128)(2,1)} slice(bf16[8192,1024]{1,0:T(8,128)(2,1)} %all-gather.7.cloned.1.call-done), slice={[0:6144], [0:1024]} | slice | bytes 25165824 | tf_op jit(solution)/shard_map/slice | solution.py:400
  958.8 44.6 %fusion.3 = (f32[6,1024,1024]{2,1,0:T(8,128)}, f32[6,1024,1024]{2,1,0:T(8,128)}) fusion(f32[6,2,16,32,1024]{4,3,2,1,0:T(8,128)} %copy.97, f32[6,1024,1024]{2,1,0:T(8,128)} %param.12, pred[6]{0:T(512)(128)(4,1)S(1)} %dynamic_slice.132, f32[6,1024,1024]{2,1,0:T(8,128)} %param.11, bf16[6,1024,1024]{2,1,0:T(8,128)(2,1)} %bitcast.338), kind=kLoop, calls=%fused_computation.6 | loop fusion | flops 50331648 | bytes 138412032 | tf_op jit(solution)/shard_map/add | solution.py:385
  (189 shorter events, 153.1 us)
Async XLA Ops:
  7.2 56.6 %all-gather.5.cloned.1.call-start = ((), (), s32[]{:S(2)}) async-start(), calls=%async_computation.4 | async-start | bytes 37748736 | tf_op jit(solution)/shard_map/all_gather | solution.py:254
  20.6 24.1 %copy-start.25 = (f32[12,1024]{1,0:T(8,128)S(1)}, f32[12,1024]{1,0:T(8,128)}, u32[]{:S(2)}) copy-start(f32[12,1024]{1,0:T(8,128)} %param.13) | copy-start | bytes 147460
  20.6 43.2 %copy-start.22 = (bf16[512,1024]{1,0:T(8,128)(2,1)S(1)}, bf16[512,1024]{1,0:T(8,128)(2,1)}, u32[]{:S(2)}) copy-start(bf16[512,1024]{1,0:T(8,128)(2,1)} %param.8) | copy-start | bytes 3145732
  20.6 348.2 %reduce-scatter.3.cloned.1.call-start = ((), (), s32[]{:S(2)}) async-start(), calls=%async_computation.5 | async-start | bytes 4456448 | tf_op jit(solution)/shard_map/reduce_scatter | solution.py:331
  69.9 9.1 copy-start.15
  128.3 23.1 %copy-start.8 = (bf16[512,1024]{1,0:T(8,128)(2,1)}, bf16[512,1024]{1,0:T(8,128)(2,1)S(1)}, u32[]{:S(2)}) copy-start(bf16[512,1024]{1,0:T(8,128)(2,1)S(1)} %get-tuple-element.143) | copy-start | bytes 3145732
  136.8 8.8 copy-start.18
  156.0 20.4 %copy-start.31 = (f32[512]{0:T(512)}, f32[512]{0:T(512)S(1)}, u32[]{:S(2)}) copy-start(f32[512]{0:T(512)S(1)} %negate_multiply_fusion) | copy-start | bytes 6148
  157.5 18.9 %copy-start.2 = (bf16[512,1024]{1,0:T(8,128)(2,1)}, bf16[512,1024]{1,0:T(8,128)(2,1)S(1)}, u32[]{:S(2)}) copy-start(bf16[512,1024]{1,0:T(8,128)(2,1)S(1)} %add_convert_fusion.6) | copy-start | bytes 3145732
  180.7 8.7 copy-start.24
  189.2 38.9 %collective-permute-start = (bf16[16,8,32,1024]{3,2,1,0:T(8,128)(2,1)}, bf16[16,8,32,1024]{3,2,1,0:T(8,128)(2,1)S(1)}, u32[]{:S(2)}, u32[]{:S(2)}) collective-permute-start(bf16[16,8,32,1024]{3,2,1,0:T(8,128)(2,1)} %dynamic-slice_bitcast_fusion), channel_id=1, source_target_pairs={{0,1},{1,0},{2,3},{3,2},{4,5},{5,4},{6,7},{7,6},{8,9},{9,8},{10,11... | collective-permute-start | bytes 25165832 | tf_op jit(solution)/shard_map/ppermute | solution.py:233
  201.9 11.7 %copy-start.16 = (bf16[1024,512]{1,0:T(8,128)(2,1)S(1)}, bf16[1024,512]{1,0:T(8,128)(2,1)}, u32[]{:S(2)}) copy-start(bf16[1024,512]{1,0:T(8,128)(2,1)} %copy-done.15) | copy-start | bytes 3145732
  257.7 10.1 %copy-start.4 = (bf16[32,4,32,1024]{3,2,1,0:T(8,128)(2,1)S(1)}, bf16[32,4,32,1024]{3,2,1,0:T(8,128)(2,1)}, u32[]{:S(2)}) copy-start(bf16[32,4,32,1024]{3,2,1,0:T(8,128)(2,1)} %weight_grads.3) | copy-start | bytes 25165828
  260.6 7.2 collective-permute-start.1
  272.2 23.8 %copy-start.20 = (bf16[512,1024]{1,0:T(8,128)(2,1)S(1)}, bf16[512,1024]{1,0:T(8,128)(2,1)}, u32[]{:S(2)}) copy-start(bf16[512,1024]{1,0:T(8,128)(2,1)} %copy-done.19) | copy-start | bytes 3145732
  272.2 276.9 %reduce-scatter.5.cloned.1.call-start = ((), (), s32[]{:S(2)}) async-start(), calls=%async_computation.6 | async-start | bytes 8912896 | tf_op jit(solution)/shard_map/reduce_scatter | solution.py:313
  272.9 26.2 %copy-start.9 = (bf16[512,1024]{1,0:T(8,128)(2,1)S(1)}, bf16[512,1024]{1,0:T(8,128)(2,1)}, u32[]{:S(2)}) copy-start(bf16[512,1024]{1,0:T(8,128)(2,1)} %copy-done.8) | copy-start | bytes 3145732
  273.0 482.2 %all-gather.9.cloned.1.call-start = ((), (), s32[]{:S(2)}) async-start(), calls=%async_computation.8 | async-start | bytes 13926400 | tf_op jit(solution)/shard_map/all_gather | solution.py:377
  368.8 183.0 %copy-start.1 = (bf16[1,4,32,1024]{3,2,1,0:T(8,128)(2,1)S(1)}, bf16[1,4,32,1024]{3,2,1,0:T(8,128)(2,1)}, u32[]{:S(2)}) copy-start(bf16[1,4,32,1024]{3,2,1,0:T(8,128)(2,1)} %reduce-scatter.3.cloned.1.call-done) | copy-start | bytes 786436
  568.4 78.9 %all-to-all-start.1 = ((bf16[16,2,32,1024]{3,2,1,0:T(8,128)(2,1)}), bf16[16,2,32,1024]{3,2,1,0:T(8,128)(2,1)S(1)}, u32[]{:S(2)}, u32[]{:S(2)}) async-start(bf16[16,2,32,1024]{3,2,1,0:T(8,128)(2,1)} %constant_dynamic-update-slice_fusion.12), calls=%async_computation.3 | async-start | bytes 4194304 | tf_op jit(solution)/shard_map/all_to_all | solution.py:393
  576.4 371.8 %all-gather.7.cloned.1.call-start = ((), (), s32[]{:S(2)}) async-start(), calls=%async_computation.7 | async-start | bytes 17825792 | tf_op jit(solution)/shard_map/all_gather | solution.py:400
  764.6 9.8 copy-start.26
  764.6 9.8 copy-start.29
  764.6 9.8 copy-start.30
  (20 other events, 56.8 us)
Sparse Core Ops, SparseCore 0:
  20.7 42.9 all-gather.4
  272.3 96.4 reduce-scatter.2
  371.6 177.4 reduce-scatter.4
  557.9 197.2 all-gather.8
  758.3 189.8 all-gather.6

commit v3 on v2

--- a/solution.py
+++ b/solution.py
@@ -215,23 +215,13 @@
     )(left, right)
 
 
-def chip_sum(pieces, piece_rows):
-    owners = lax.axis_size("own")
+def scatter_sum(pieces, piece_rows, devices):
     kernel_rows = pieces.shape[2]
     if kernel_rows != piece_rows:
         finer = kernel_rows // piece_rows
         pieces = pieces.reshape(pieces.shape[0], -1, finer, piece_rows, pieces.shape[3])
-        pieces = pieces.transpose(0, 2, 1, 3, 4).reshape(
-            pieces.shape[0] * finer, -1, piece_rows, pieces.shape[4]
-        )
-    if owners != 2:
-        return lax.psum_scatter(pieces, "own", scatter_dimension=0, tiled=True)
-    halves = pieces.reshape((owners, -1) + pieces.shape[1:])
-    me = lax.axis_index("own")
-    kept = lax.dynamic_index_in_dim(halves, me, 0, keepdims=False)
-    sent = lax.dynamic_index_in_dim(halves, 1 - me, 0, keepdims=False)
-    got = lax.ppermute(sent, "own", [(0, 1), (1, 0)])
-    return (kept.astype(jnp.float32) + got.astype(jnp.float32)).astype(jnp.bfloat16)
+        pieces = pieces.transpose(0, 2, 1, 3, 4).reshape(devices, -1, piece_rows, pieces.shape[4])
+    return lax.psum_scatter(pieces, ("dp", "own"), scatter_dimension=0, tiled=True)[0]
 
 
 def on_device(
@@ -309,15 +299,11 @@
         kernel_rows,
     )
     d_attn, feed_pieces = lax.optimization_barrier((d_attn, feed_pieces))
-    feed_sum = chip_sum(feed_pieces, piece_rows)
-    feed_share = lax.psum_scatter(feed_sum, "dp", scatter_dimension=0, tiled=True)[0]
+    feed_share = scatter_sum(feed_pieces, piece_rows, devices)
     d_mixed = contract_last(d_attn, w_out).astype(jnp.bfloat16)
     bundle = triples + (d_mixed.reshape(sequences, LEN, features), row_peak, row_total)
     d_query, d_key, d_value = (
         part.reshape(sequences * LEN, features) for part in lax.map(attend_backward, bundle)
-    )
-    d_query, d_key, d_value, feed_sum = lax.optimization_barrier(
-        (d_query, d_key, d_value, feed_sum)
     )
     attn_pieces = weight_grads(
         jnp.stack([tokens, mixed_rows]),
@@ -327,9 +313,6 @@
         4,
         kernel_rows,
     )
-    attn_sum = chip_sum(attn_pieces, piece_rows)
-    attn_share = lax.psum_scatter(attn_sum, "dp", scatter_dimension=0, tiled=True)[0]
-    share = jnp.concatenate([attn_share, feed_share], axis=0)
     input_grad = (
         d_resid_one
         + contract_last(d_query, w_query)
@@ -352,7 +335,12 @@
         ]
         + [column_sum(part) for part in d_hidden]
     )
-    vector_chip = lax.psum(vector_local, "own").astype(jnp.bfloat16)
+    vector_grad = lax.psum(vector_local, ("dp", "own"))
+    attn_pieces, feed_share, vector_grad = lax.optimization_barrier(
+        (attn_pieces, feed_share, vector_grad)
+    )
+    attn_share = scatter_sum(attn_pieces, piece_rows, devices)
+    share = jnp.concatenate([attn_share, feed_share], axis=0)
 
     match = slot_table[None, :] == jnp.arange(slot_count, dtype=jnp.int32)[:, None]
     slot_used = jnp.any(match, axis=1)
@@ -363,23 +351,8 @@
         [lax.dynamic_index_in_dim(share, block_index[s], 0, keepdims=False) for s in range(slot_count)]
     ).reshape(owners, slots, piece_rows, features)
     mine = lax.all_to_all(slot_share, "own", split_axis=0, concat_axis=0, tiled=True)
-    rows_here = owners * slots * piece_rows
-    vector_rows = vector_chip.shape[0]
-    padded = -(-(rows_here + vector_rows) // 16) * 16
-    outgoing = jnp.concatenate(
-        [
-            mine.reshape(rows_here, features),
-            vector_chip,
-            jnp.zeros((padded - rows_here - vector_rows, features), jnp.bfloat16),
-        ],
-        axis=0,
-    )
-    incoming = lax.all_gather(outgoing, "dp", axis=0, tiled=False)
-    vector_grad = jnp.sum(
-        incoming[:, rows_here : rows_here + vector_rows].astype(f32), axis=0
-    )
-    summed = incoming[:, :rows_here].reshape(data_count, owners, slots, piece_rows, features)
-    summed = summed.transpose(2, 1, 0, 3, 4).reshape(slots, features, features).astype(f32)
+    summed = lax.all_gather(mine, "dp", axis=0, tiled=False)
+    summed = summed.transpose(2, 0, 1, 3, 4).reshape(slots, features, features).astype(f32)
     used_here = lax.dynamic_slice_in_dim(slot_used, lax.axis_index("own") * slots, slots)
     used_here = used_here[:, None, None]
     new_momentum = momentum_decay * matrix_momentum + jnp.where(used_here, summed, 0.0)
@@ -391,13 +364,15 @@
     place_of = [min(index // copies, slots - 1) for index in range(data_count)]
     by_turn = jnp.stack([mine[:, place] for place in place_of])
     my_rows = lax.all_to_all(by_turn, "dp", split_axis=0, concat_axis=0, tiled=True)
-    my_summed = my_rows.transpose(1, 0, 2, 3).reshape(features, features).astype(f32)
+    my_summed = my_rows.reshape(features, features).astype(f32)
     slot_place = jnp.minimum(turn // copies, slots - 1)
     my_momentum = lax.dynamic_index_in_dim(matrix_momentum, slot_place, 0, keepdims=False)
     ortho_low = orthogonal(momentum_decay * my_momentum + my_summed)
     part_rows = features // copies
     ortho_part = lax.dynamic_slice_in_dim(ortho_low, (turn % copies) * part_rows, part_rows, 0)
-    ortho = lax.all_gather(ortho_part, "dp", axis=0, tiled=True)[: slots * features]
+    ortho = lax.all_gather(ortho_part, "dp", axis=0, tiled=True)
+    ortho, new_momentum = lax.optimization_barrier((ortho, new_momentum))
+    ortho = ortho[: slots * features]
     ortho = jnp.where(used_here, ortho.reshape(slots, features, features).astype(f32), 0.0)
     new_master = matrix_master - matrix_rate * (ortho + matrix_decay * matrix_master)
     new_first = beta_first * vector_first + (1.0 - beta_first) * vector_grad

time: 1020 us -> 935 us (0.917)
  waiting for transfers between devices: 561 us -> 477 us
  blocking collectives: 8.13 us -> 48.1 us
  local copies, waits for them, and re-layouts: 64.6 us -> 45.2 us
  other arithmetic: 112 us -> 93.6 us
    reduce_scatter x2, waiting for transfers between devices: 245 us -> 205 us  [scatter_sum(): lax.psum_scatter(pieces, ('dp', 'own'), scatter_dimension=0, tiled=True)[0]]
    psum x1, blocking collectives: 3.76 us -> 43 us  [on_device(): vector_grad = lax.psum(vector_local, ('dp', 'own'))]
    all_gather x2, waiting for transfers between devices: 218 us -> 190 us  [the longest x1 151 us: on_device(): ortho = lax.all_gather(ortho_part, 'dp', axis=0, tiled=True)]
    sub x0 -> x1, other arithmetic: none -> 19.3 us  [on_device(): matrix_master - matrix_rate * (ortho + matrix_decay * matrix_master)]
    add x1, other arithmetic: 44.6 us -> 25.5 us  [on_device(): momentum_decay * matrix_momentum + jnp.where(used_here, summed, 0.0)]
    slice x2, local copies, waits for them, and re-layouts: 16.8 us -> 4.58 us  [on_device(): ortho = ortho[:slots * features]]
    squeeze x2 -> x0, local copies, waits for them, and re-layouts: 11.4 us -> none  [chip_sum(): sent = lax.dynamic_index_in_dim(halves, 1 - me, 0, keepdims=False)]
    unnamed x87 -> x101, local copies, waits for them, and re-layouts: 16 us -> 21.2 us
  transfers between devices with their start and end apart: 8 -> 6, of which waited for: 7 -> 6; matrix products, arithmetic and copies ran while one was open for 9% -> 14% of each run, Pallas kernels for 4% -> 6%
where the time goes in v3:
time: 935 us; the launch traced here: 927 us
  waiting for transfers between devices  477 us (51%)
  matrix products  126 us (13%)
  other arithmetic  93.6 us (10%)
  Pallas kernels  73.4 us (8%)
  between operations  60.5 us (6%)
  blocking collectives  48.1 us (5%)
  local copies, waits for them, and re-layouts  45.2 us (5%)
    reduce_scatter x2, waiting for transfers between devices, scatter_sum(): lax.psum_scatter(pieces, ('dp', 'own'), scatter_dimension=0, tiled=True)[0]  205 us
    all_gather x1, waiting for transfers between devices, on_device(): ortho = lax.all_gather(ortho_part, 'dp', axis=0, tiled=True)  151 us
    all_to_all x1, waiting for transfers between devices, on_device(): lax.all_to_all(by_turn, 'dp', split_axis=0, concat_axis=0, tiled=True)  62.9 us
    dot_general x12, matrix products, contract_last(): lax.dot_general(operand_left, operand_right, (((1,), (1,)), ((), ())), pr...  44.7 us
    pallas_call x1, Pallas kernels, orthogonal(): pl.pallas_call(newton_kernel, out_shape=jax.ShapeDtypeStruct((size, size)...  44.1 us
    psum x1, blocking collectives, on_device(): vector_grad = lax.psum(vector_local, ('dp', 'own'))  43 us
    all_gather x1, waiting for transfers between devices, on_device(): summed = lax.all_gather(mine, 'dp', axis=0, tiled=False)  39.2 us
    dot_general x12, matrix products, dot(): return jnp.dot(left, right, preferred_element_type=f32)  36.7 us
  transfers between devices with their start and end apart: 6, of which 6 were waited for; matrix products, arithmetic and copies ran while one was open for 14% of the time, Pallas kernels for 6%

profile of v3, /device:TPU:0, one launch (start us, length us, event | category | flops | bytes accessed | tf_op | source)
XLA Modules:
  0.0 927.2 jit_solution(14319102601684955442)
XLA Ops:
  7.2 13.3 %convert_element_type.209 = bf16[6,1024,1024]{2,1,0:T(8,128)(2,1)} convert(f32[6,1024,1024]{2,1,0:T(8,128)} %param.11) | non-fusion elementwise | flops 6291456 | bytes 37748736 | tf_op jit(solution)/shard_map/convert_element_type | solution.py:244
  44.9 18.9 %all-gather.5.cloned.1.call-done = bf16[12,1024,1024]{2,1,0:T(8,128)(2,1)} async-done(((bf16[6,1024,1024]{2,1,0:T(8,128)(2,1)}), bf16[12,1024,1024]{2,1,0:T(8,128)(2,1)}) %all-gather.5.cloned.1.call-update) | async-done | bytes 25165840 | tf_op jit(solution)/shard_map/all_gather | solution.py:244
  69.9 9.2 fusion.181
  82.2 7.7 fusion.97
  156.5 18.4 %weight_grads.2 = bf16[32,8,32,1024]{3,2,1,0:T(8,128)(2,1)} custom-call(bf16[5,512,1024]{2,1,0:T(8,128)(2,1)S(1)} %get-tuple-element.83.left_ref, bf16[5,512,1024]{2,1,0:T(8,128)(2,1)} %copy-done.41), custom_call_target="tpu_custom_call" | custom-call | flops 8589934592 | bytes 25165824 | tf_op jit(solution)/shard_map/weight_grads/pallas_call | solution.py:199
  180.3 9.1 convert_reduce_fusion.7
  191.6 10.2 %multiply_reduce_fusion = (f32[16,512]{1,0:T(8,128)}, f32[16,512,512]{1,2,0:T(8,128)S(1)}) fusion(f32[16,512,512]{1,2,0:T(8,128)} %get-tuple-element.133, f32[16,512]{1,0:T(8,128)} %copy-done.34, bf16[512,16,64]{0,2,1:T(8,128)(2,1)} %bitcast.353, bf16[512,16,64]{0,2,1:T(8,128)(2,1)} %bitcast.389), kind=kOutput, calls=%fused_computation.8 | convolution fusion | flops 549445632 | bytes 35717120 | tf_op jit(solution)/shard_map/while/body/eval_jaxpr/qhd,khd->hqk/dot_general | solution.py:84
  201.8 8.1 multiply_convert_fusion
  213.4 6.7 multiply_convert_fusion.1
  226.6 43.0 %psum.7 = f32[12,1024]{1,0:T(8,128)S(1)} all-reduce(f32[12,1024]{1,0:T(8,128)S(1)} %stack.121), channel_id=1, replica_groups=mesh['dp'=16,'own'=2] {'dp','own'}, use_global_device_ids=true, to_apply=%region_25.26 | all-reduce | flops 12288 | bytes 98304 | tf_op jit(solution)/shard_map/psum | solution.py:338
  274.0 10.9 %weight_grads.3 = bf16[32,4,32,1024]{3,2,1,0:T(8,128)(2,1)} custom-call(bf16[2,512,1024]{2,1,0:T(8,128)(2,1)S(1)} %pad_maximum_fusion.1.left_ref, bf16[4,512,1024]{2,1,0:T(8,128)(2,1)} %pad_maximum_fusion.right_ref), custom_call_target="tpu_custom_call" | custom-call | flops 4294967296 | bytes 12582912 | tf_op jit(solution)/shard_map/weight_grads/pallas_call | solution.py:199
  284.9 75.6 %reduce-scatter.3.cloned.1.call-done = bf16[1,8,32,1024]{3,2,1,0:T(8,128)(2,1)} async-done(((bf16[32,8,32,1024]{3,2,1,0:T(8,128)(2,1)}), bf16[1,8,32,1024]{3,2,1,0:T(8,128)(2,1)}) %reduce-scatter.3.cloned.1.call-update) | async-done | bytes 524304 | tf_op jit(solution)/shard_map/reduce_scatter | solution.py:224
  384.8 129.1 %reduce-scatter.5.cloned.1.call-done = bf16[1,4,32,1024]{3,2,1,0:T(8,128)(2,1)} async-done(((bf16[32,4,32,1024]{3,2,1,0:T(8,128)(2,1)}), bf16[1,4,32,1024]{3,2,1,0:T(8,128)(2,1)}) %reduce-scatter.5.cloned.1.call-update) | async-done | bytes 262160 | tf_op jit(solution)/shard_map/reduce_scatter | solution.py:224
  515.3 5.2 all_to_all.10
  539.6 62.9 %all-to-all-done.1 = bf16[16,2,32,1024]{3,2,1,0:T(8,128)(2,1)S(1)} async-done(((bf16[16,2,32,1024]{3,2,1,0:T(8,128)(2,1)}), bf16[16,2,32,1024]{3,2,1,0:T(8,128)(2,1)S(1)}, u32[]{:S(2)}, u32[]{:S(2)}) %all-to-all-start.1) | async-done | bytes 2097184 | tf_op jit(solution)/shard_map/all_to_all | solution.py:366
  602.5 5.3 convert_add_fusion.momentum_ref
  607.7 44.1 %newton.1 = bf16[1024,1024]{1,0:T(8,128)(2,1)S(1)} custom-call(f32[1024,1024]{1,0:T(8,128)} %convert_add_fusion.momentum_ref), custom_call_target="tpu_custom_call" | custom-call | flops 32212254720 | bytes 6291456 | tf_op jit(solution)/shard_map/newton/pallas_call | solution.py:170
  659.6 4.6 add_add_fusion.2
  664.9 39.2 %all-gather.9.cloned.1.call-done = bf16[32,6,32,1024]{3,2,1,0:T(8,128)(2,1)} async-done(((bf16[2,6,32,1024]{3,2,1,0:T(8,128)(2,1)}), bf16[32,6,32,1024]{3,2,1,0:T(8,128)(2,1)}) %all-gather.9.cloned.1.call-update) | async-done | bytes 12582928 | tf_op jit(solution)/shard_map/all_gather | solution.py:354
  704.0 7.2 convert_bitcast_fusion
  711.2 9.1 copy.80
  720.3 25.5 %fusion.3 = f32[6,1024,1024]{2,1,0:T(8,128)} fusion(f32[6,16,2,32,1024]{4,3,2,1,0:T(8,128)} %copy.80, f32[6,1024,1024]{2,1,0:T(8,128)} %param.12, pred[6]{0:T(512)(128)(4,1)S(1)} %dynamic_slice.116), kind=kLoop, calls=%fused_computation.6 | loop fusion | flops 18874368 | bytes 75497480 | tf_op jit(solution)/shard_map/add | solution.py:358
  745.8 150.8 %all-gather.7.cloned.1.call-done = bf16[8192,1024]{1,0:T(8,128)(2,1)} async-done(((bf16[512,1024]{1,0:T(8,128)(2,1)}), bf16[8192,1024]{1,0:T(8,128)(2,1)}) %all-gather.7.cloned.1.call-update) | async-done | bytes 16777232 | tf_op jit(solution)/shard_map/all_gather | solution.py:373
  901.1 19.3 %fusion.2 = f32[6,1024,1024]{2,1,0:T(8,128)} fusion(f32[6,1024,1024]{2,1,0:T(8,128)} %param.11, bf16[6,1024,1024]{2,1,0:T(8,128)(2,1)S(1)} %bitcast.325, pred[6]{0:T(512)(128)(4,1)S(1)} %dynamic_slice.116), kind=kLoop, calls=%fused_computation.3 | loop fusion | flops 31457280 | bytes 62914568 | tf_op jit(solution)/shard_map/sub | solution.py:377
  (191 shorter events, 133.4 us)
Async XLA Ops:
  7.2 56.6 %all-gather.5.cloned.1.call-start = ((), (), s32[]{:S(2)}) async-start(), calls=%async_computation.4 | async-start | bytes 37748736 | tf_op jit(solution)/shard_map/all_gather | solution.py:244
  20.6 24.2 %copy-start.28 = (f32[12,1024]{1,0:T(8,128)S(1)}, f32[12,1024]{1,0:T(8,128)}, u32[]{:S(2)}) copy-start(f32[12,1024]{1,0:T(8,128)} %param.13) | copy-start | bytes 147460
  20.6 43.2 %copy-start.27 = (bf16[512,1024]{1,0:T(8,128)(2,1)S(1)}, bf16[512,1024]{1,0:T(8,128)(2,1)}, u32[]{:S(2)}) copy-start(bf16[512,1024]{1,0:T(8,128)(2,1)} %param.8) | copy-start | bytes 3145732
  20.6 339.9 %reduce-scatter.3.cloned.1.call-start = ((), (), s32[]{:S(2)}) async-start(), calls=%async_computation.5 | async-start | bytes 17301504 | tf_op jit(solution)/shard_map/reduce_scatter | solution.py:224
  69.9 9.3 %copy-start.19 = (bf16[1024,512]{1,0:T(8,128)(2,1)}, bf16[1024,512]{1,0:T(8,128)(2,1)S(1)}, u32[]{:S(2)}) copy-start(bf16[1024,512]{1,0:T(8,128)(2,1)S(1)} %add_convert_fusion.4) | copy-start | bytes 3145732
  82.1 7.8 copy-start.42
  126.7 23.1 %copy-start.10 = (bf16[512,1024]{1,0:T(8,128)(2,1)}, bf16[512,1024]{1,0:T(8,128)(2,1)S(1)}, u32[]{:S(2)}) copy-start(bf16[512,1024]{1,0:T(8,128)(2,1)S(1)} %get-tuple-element.145) | copy-start | bytes 3145732
  131.0 8.6 copy-start.22
  135.2 8.8 copy-start.24
  139.5 7.5 copy-start.25
  155.0 19.9 %copy-start.39 = (f32[512]{0:T(512)}, f32[512]{0:T(512)S(1)}, u32[]{:S(2)}) copy-start(f32[512]{0:T(512)S(1)} %negate_multiply_fusion) | copy-start | bytes 6148
  175.0 338.9 %reduce-scatter.5.cloned.1.call-start = ((), (), s32[]{:S(2)}) async-start(), calls=%async_computation.6 | async-start | bytes 8650752 | tf_op jit(solution)/shard_map/reduce_scatter | solution.py:224
  180.1 9.3 %copy-start.26 = (bf16[512,1024]{0,1:T(8,128)(2,1)}, bf16[512,1024]{0,1:T(8,128)(2,1)S(1)}, u32[]{:S(2)}) copy-start(bf16[512,1024]{0,1:T(8,128)(2,1)S(1)} %copy.67) | copy-start | bytes 3145732
  201.8 8.1 copy-start.18
  213.3 8.1 copy-start.6
  224.4 45.2 %copy-start.13 = (bf16[1,512,1024]{2,1,0:T(8,128)(2,1)S(1)}, bf16[1,512,1024]{2,1,0:T(8,128)(2,1)}, u32[]{:S(2)}) copy-start(bf16[1,512,1024]{2,1,0:T(8,128)(2,1)} %copy.71) | copy-start | bytes 3145732
  360.5 153.4 %copy-start.1 = (bf16[1,8,32,1024]{3,2,1,0:T(8,128)(2,1)S(1)}, bf16[1,8,32,1024]{3,2,1,0:T(8,128)(2,1)}, u32[]{:S(2)}) copy-start(bf16[1,8,32,1024]{3,2,1,0:T(8,128)(2,1)} %reduce-scatter.3.cloned.1.call-done) | copy-start | bytes 1572868
  360.5 343.5 %all-gather.9.cloned.1.call-start = ((), (), s32[]{:S(2)}) async-start(), calls=%async_computation.8 | async-start | bytes 13369344 | tf_op jit(solution)/shard_map/all_gather | solution.py:354
  520.5 8.0 copy-start.3
  535.8 66.7 %all-to-all-start.1 = ((bf16[16,2,32,1024]{3,2,1,0:T(8,128)(2,1)}), bf16[16,2,32,1024]{3,2,1,0:T(8,128)(2,1)S(1)}, u32[]{:S(2)}, u32[]{:S(2)}) async-start(bf16[16,2,32,1024]{3,2,1,0:T(8,128)(2,1)} %constant_dynamic-update-slice_fusion.12), calls=%async_computation.3 | async-start | bytes 4194304 | tf_op jit(solution)/shard_map/all_to_all | solution.py:366
  539.5 357.0 %all-gather.7.cloned.1.call-start = ((), (), s32[]{:S(2)}) async-start(), calls=%async_computation.7 | async-start | bytes 17825792 | tf_op jit(solution)/shard_map/all_gather | solution.py:373
  659.5 4.6 copy-start.29
  659.6 4.6 copy-start.32
  659.6 4.6 copy-start.33
  (26 other events, 60.2 us)
Sparse Core Ops, SparseCore 0:
  20.7 42.9 all-gather.4
  175.1 185.3 reduce-scatter.2
  363.4 150.4 reduce-scatter.4
  520.7 183.3 all-gather.8
  706.7 189.8 all-gather.6
